TPU v7x, 32 devices: a whole 2x2x4 slice. The times are simulated.
32 devices in a mesh: dp: 8 (over z, y), ctx: 4 (over x, core).
Axes of the slice: x: 2, y: 2, z: 4, core: 2. Of those that a mesh axis runs over, the one named last changes fastest.
Arguments:
- tokens: bfloat16 [8, 1024, 768], P('dp', 'ctx'), may hold values from -6 to 6
- segments: int32 [8, 1024], P('dp', 'ctx'), may hold values from 0 to 2, as said below
- ln1_gain: bfloat16 [2, 768], P(None, ('dp', 'ctx')), may hold values from 0.5 to 1.5
- ln1_bias: bfloat16 [2, 768], P(None, ('dp', 'ctx')), may hold values from -1.75 to 1.75
- w_query: bfloat16 [2, 768, 768], P(None, ('dp', 'ctx')), may hold values from -0.21875 to 0.21875
- b_query: bfloat16 [2, 768], P(None, ('dp', 'ctx')), may hold values from -3 to 3
- w_key: bfloat16 [2, 768, 768], P(None, ('dp', 'ctx')), may hold values from -0.21875 to 0.21875
- w_value: bfloat16 [2, 768, 768], P(None, ('dp', 'ctx')), may hold values from -0.21875 to 0.21875
- b_value: bfloat16 [2, 768], P(None, ('dp', 'ctx')), may hold values from -0.3125 to 0.3125
- w_out: bfloat16 [2, 768, 768], P(None, ('dp', 'ctx')), may hold values from -1.75 to 1.75
- b_out: bfloat16 [2, 768], P(None, ('dp', 'ctx')), may hold values from -1.75 to 1.75
- ln2_gain: bfloat16 [2, 768], P(None, ('dp', 'ctx')), may hold values from 0.5 to 1.5
- ln2_bias: bfloat16 [2, 768], P(None, ('dp', 'ctx')), may hold values from -1.75 to 1.75
- w_up: bfloat16 [2, 768, 3072], P(None, ('dp', 'ctx')), may hold values from -0.21875 to 0.21875
- b_up: bfloat16 [2, 3072], P(None, ('dp', 'ctx')), may hold values from -3 to 3
- w_down: bfloat16 [2, 3072, 768], P(None, ('dp', 'ctx')), may hold values from -0.109375 to 0.109375
- b_down: bfloat16 [2, 768], P(None, ('dp', 'ctx')), may hold values from -1.75 to 1.75
- out_grad: bfloat16 [8, 1024, 768], P('dp', 'ctx'), may hold values from -6 to 6
Outputs:
- output: bfloat16 [8, 1024, 768], P('dp', 'ctx')
- input_grad: float32 [8, 1024, 768], P('dp', 'ctx')
- grad_ln1_gain: float32 [2, 768], P(None, ('dp', 'ctx'))
- grad_ln1_bias: float32 [2, 768], P(None, ('dp', 'ctx'))
- grad_w_query: float32 [2, 768, 768], P(None, ('dp', 'ctx'))
- grad_b_query: float32 [2, 768], P(None, ('dp', 'ctx'))
- grad_w_key: float32 [2, 768, 768], P(None, ('dp', 'ctx'))
- grad_w_value: float32 [2, 768, 768], P(None, ('dp', 'ctx'))
- grad_b_value: float32 [2, 768], P(None, ('dp', 'ctx'))
- grad_w_out: float32 [2, 768, 768], P(None, ('dp', 'ctx'))
- grad_b_out: float32 [2, 768], P(None, ('dp', 'ctx'))
- grad_ln2_gain: float32 [2, 768], P(None, ('dp', 'ctx'))
- grad_ln2_bias: float32 [2, 768], P(None, ('dp', 'ctx'))
- grad_w_up: float32 [2, 768, 3072], P(None, ('dp', 'ctx'))
- grad_b_up: float32 [2, 3072], P(None, ('dp', 'ctx'))
- grad_w_down: float32 [2, 3072, 768], P(None, ('dp', 'ctx'))
- grad_b_down: float32 [2, 768], P(None, ('dp', 'ctx'))
Inputs may be any that keep to these rules, and one draw needn't show every extreme that they name: `segments`: in each sequence the document numbers never fall. Document 1 begins after position 0 and within the first 256 positions, and ends within the last 256 positions; document 0 is never empty, document 2 may be.
All inputs are finite; a program needn't handle non-finite values.
Results may differ from a plain program's by a relative error of at most 0.025.
Values may be sent and summed in bfloat16 or wider, within the bound.
A program may use at most 320 MiB of HBM per device.

v0:
```python
import jax
import jax.numpy as jnp
from jax import lax
from jax.sharding import PartitionSpec as P

H = 12
HD = 64


EPSILON = 1e-05
MASKED = -1e30


def matmul(left_op, right_op):
    return jnp.dot(left_op, right_op, preferred_element_type=jnp.float32)


def contract_rows(left_op, right_op):
    return lax.dot_general(
        left_op, right_op, (((0,), (0,)), ((), ())), preferred_element_type=jnp.float32
    )


def contract_cols(left_op, right_op):
    return lax.dot_general(
        left_op, right_op, (((1,), (1,)), ((), ())), preferred_element_type=jnp.float32
    )


def normalize(values):
    centre = jnp.mean(values, axis=-1, keepdims=True)
    centred = values - centre
    scale_vec = lax.rsqrt(jnp.mean(centred * centred, axis=-1, keepdims=True) + EPSILON)
    return (centred * scale_vec, scale_vec)


def norm_back(grad_in, normed, scale_vec, gain_vec):
    scaled = grad_in * gain_vec
    return scale_vec * (
        scaled
        - jnp.mean(scaled, axis=-1, keepdims=True)
        - normed * jnp.mean(scaled * normed, axis=-1, keepdims=True)
    )


def attend_forward(queries, key_rows, values, seg_own, first_place):
    row_count = queries.shape[0]
    score_scale = HD ** (-0.5)
    q_heads = queries.reshape(row_count, H, HD)
    q_place = first_place + jnp.arange(row_count)
    q_seg = seg_own.astype(jnp.float32)
    last_place = first_place + row_count - 1
    first_seg = q_seg[0]
    initial = (
        jnp.full((H, row_count), MASKED, jnp.float32),
        jnp.zeros((H, row_count), jnp.float32),
        jnp.zeros((row_count, H, HD), jnp.float32),
    )
    key_piece = lax.all_gather(key_rows, "ctx", axis=0, tiled=True)
    value_piece = lax.all_gather(values, "ctx", axis=0, tiled=True)
    seg_piece = lax.all_gather(seg_own.astype(jnp.bfloat16), "ctx", axis=0, tiled=True)
    key_count = key_piece.shape[0]
    seg_keys = seg_piece.astype(jnp.float32)

    def update(current):
        highest, totals, weighted = current
        scores = (
            jnp.einsum(
                "qhd,khd->hqk",
                q_heads,
                key_piece.reshape(key_count, H, HD),
                preferred_element_type=jnp.float32,
            )
            * score_scale
        )
        k_place = jnp.arange(key_count)
        allowed = (k_place[None, :] <= q_place[:, None]) & (seg_keys[None, :] == q_seg[:, None])
        scores = jnp.where(allowed[None], scores, MASKED)
        new_high = jnp.maximum(highest, jnp.max(scores, axis=-1))
        weights = jnp.where(allowed[None], jnp.exp(scores - new_high[:, :, None]), 0.0)
        totals = jnp.sum(weights, axis=-1)
        weighted = jnp.einsum(
            "hqk,khd->qhd",
            weights.astype(jnp.bfloat16),
            value_piece.reshape(key_count, H, HD),
            preferred_element_type=jnp.float32,
        )
        return (new_high, totals, weighted)

    reaches = (jnp.int32(0) <= last_place) & (seg_keys[key_count - 1] >= first_seg)
    highest, totals, weighted = lax.cond(reaches, update, lambda current: current, initial)
    mixed_out = weighted / jnp.transpose(totals)[:, :, None]
    return (mixed_out.reshape(row_count, H * HD), highest + jnp.log(totals))


def block_shape(seq_len, row_count):
    shard_count = seq_len // row_count
    shards_per = max(1, min(shard_count, 512 // row_count))
    while shard_count % shards_per != 0:
        shards_per -= 1
    block_len = shards_per * row_count
    return (block_len, seq_len // block_len)


def attend_back(queries, mixed_out, grad_mixed, log_total, key_rows, values, seg_own, first_place):
    row_count = queries.shape[0]
    score_scale = HD ** (-0.5)
    q_heads = queries.reshape(row_count, H, HD)
    q_place = first_place + jnp.arange(row_count)
    q_seg = seg_own.astype(jnp.float32)
    last_place = first_place + row_count - 1
    first_seg = q_seg[0]
    all_keys, all_values, all_segs = (
        lax.all_gather(key_rows, "ctx", axis=0, tiled=True),
        lax.all_gather(values, "ctx", axis=0, tiled=True),
        lax.all_gather(seg_own.astype(jnp.bfloat16), "ctx", axis=0, tiled=True),
    )
    seq_len = all_keys.shape[0]
    block_len, blocks = block_shape(seq_len, row_count)
    grad_heads = grad_mixed.reshape(row_count, H, HD)
    row_delta = jnp.transpose(
        jnp.sum(grad_heads.astype(jnp.float32) * mixed_out.reshape(row_count, H, HD), axis=-1)
    )
    block_inputs = (
        all_keys.reshape(blocks, block_len, H * HD),
        all_values.reshape(blocks, block_len, H * HD),
        all_segs.reshape(blocks, block_len),
        jnp.arange(blocks, dtype=jnp.int32) * block_len,
    )

    def block_terms(key_blk, value_blk, seg_keys, offset):
        key_heads = key_blk.reshape(block_len, H, HD)
        val_heads = value_blk.reshape(block_len, H, HD)
        scores = (
            jnp.einsum("qhd,khd->hqk", q_heads, key_heads, preferred_element_type=jnp.float32)
            * score_scale
        )
        k_place = offset + jnp.arange(block_len)
        allowed = (k_place[None, :] <= q_place[:, None]) & (seg_keys[None, :] == q_seg[:, None])
        scores = jnp.where(allowed[None], scores, MASKED)
        probs_block = jnp.where(allowed[None], jnp.exp(scores - log_total[:, :, None]), 0.0)
        grad_p = jnp.einsum(
            "qhd,khd->hqk", grad_heads, val_heads, preferred_element_type=jnp.float32
        )
        grad_s = (probs_block * (grad_p - row_delta[:, :, None])).astype(jnp.bfloat16)
        return (key_heads, probs_block, grad_s)

    def query_grad_step(grad_q, block_data):
        key_blk, value_blk, seg_blk, offset = block_data
        seg_keys = seg_blk.astype(jnp.float32)

        def query_compute(grad_run):
            key_heads, probs_block, grad_s = block_terms(key_blk, value_blk, seg_keys, offset)
            return (
                grad_run
                + jnp.einsum("hqk,khd->qhd", grad_s, key_heads, preferred_element_type=jnp.float32)
                * score_scale
            )

        reaches = (offset <= last_place) & (seg_keys[block_len - 1] >= first_seg)
        return (lax.cond(reaches, query_compute, lambda grad_run: grad_run, grad_q), None)

    grad_q, unused = lax.scan(
        query_grad_step, jnp.zeros((row_count, H, HD), jnp.float32), block_inputs
    )
    all_queries, all_gmix, all_qsegs = (
        lax.all_gather(queries, "ctx", axis=0, tiled=True),
        lax.all_gather(grad_mixed, "ctx", axis=0, tiled=True),
        lax.all_gather(seg_own.astype(jnp.bfloat16), "ctx", axis=0, tiled=True),
    )
    all_logs, all_deltas = (
        lax.all_gather(jnp.transpose(log_total), "ctx", axis=0, tiled=True),
        lax.all_gather(jnp.transpose(row_delta), "ctx", axis=0, tiled=True),
    )
    own_key_heads = key_rows.reshape(row_count, H, HD)
    own_val_heads = values.reshape(row_count, H, HD)
    k_place = first_place + jnp.arange(row_count)
    query_inputs = (
        all_queries.reshape(blocks, block_len, H * HD),
        all_gmix.reshape(blocks, block_len, H * HD),
        all_qsegs.reshape(blocks, block_len),
        all_logs.reshape(blocks, block_len, H),
        all_deltas.reshape(blocks, block_len, H),
        jnp.arange(blocks, dtype=jnp.int32) * block_len,
    )

    def key_grad_step(carry, block_data):
        q_blk, gmix_blk, qseg_blk, log_blk, delta_blk, offset = block_data
        qseg_rows = qseg_blk.astype(jnp.float32)

        def key_compute(current):
            grad_k, grad_v = current
            qh_blk = q_blk.reshape(block_len, H, HD)
            gh_blk = gmix_blk.reshape(block_len, H, HD)
            scores = (
                jnp.einsum(
                    "qhd,khd->hqk", qh_blk, own_key_heads, preferred_element_type=jnp.float32
                )
                * score_scale
            )
            place_rows = offset + jnp.arange(block_len)
            allowed = (k_place[None, :] <= place_rows[:, None]) & (
                q_seg[None, :] == qseg_rows[:, None]
            )
            scores = jnp.where(allowed[None], scores, MASKED)
            probs_block = jnp.where(
                allowed[None], jnp.exp(scores - jnp.transpose(log_blk)[:, :, None]), 0.0
            )
            grad_v = grad_v + jnp.einsum(
                "hqk,qhd->khd",
                probs_block.astype(jnp.bfloat16),
                gh_blk,
                preferred_element_type=jnp.float32,
            )
            grad_p = jnp.einsum(
                "qhd,khd->hqk", gh_blk, own_val_heads, preferred_element_type=jnp.float32
            )
            grad_s = (probs_block * (grad_p - jnp.transpose(delta_blk)[:, :, None])).astype(
                jnp.bfloat16
            )
            grad_k = (
                grad_k
                + jnp.einsum("hqk,qhd->khd", grad_s, qh_blk, preferred_element_type=jnp.float32)
                * score_scale
            )
            return (grad_k, grad_v)

        reaches = (offset + block_len - 1 >= first_place) & (qseg_rows[block_len - 1] >= first_seg)
        return (lax.cond(reaches, key_compute, lambda current: current, carry), None)

    zero_heads = jnp.zeros((row_count, H, HD), jnp.float32)
    (own_k, own_v), unused = lax.scan(key_grad_step, (zero_heads, zero_heads), query_inputs)
    own_keys = own_k.reshape(row_count, H * HD)
    own_values = own_v.reshape(row_count, H * HD)
    return (
        grad_q.reshape(row_count, H * HD).astype(jnp.bfloat16),
        own_keys.astype(jnp.bfloat16),
        own_values.astype(jnp.bfloat16),
    )


def layer_forward(stream, seg_own, first_place, gathered):
    (
        gain_one,
        shift_one,
        w_query,
        b_query,
        w_key,
        w_value,
        b_value,
        w_out,
        b_out,
        gain_two,
        shift_two,
        w_up,
        b_up,
        w_down,
        b_down,
    ) = gathered
    normed_one, scale_one = normalize(stream)
    inputs_one = (normed_one * gain_one + shift_one).astype(jnp.bfloat16)
    queries = (matmul(inputs_one, w_query) + b_query).astype(jnp.bfloat16)
    key_rows = matmul(inputs_one, w_key).astype(jnp.bfloat16)
    values = (matmul(inputs_one, w_value) + b_value).astype(jnp.bfloat16)
    mixed_out, log_total = attend_forward(queries, key_rows, values, seg_own, first_place)
    mixed_low = mixed_out.astype(jnp.bfloat16)
    stream_mid = stream + matmul(mixed_low, w_out) + b_out
    normed_two, scale_two = normalize(stream_mid)
    inputs_two = (normed_two * gain_two + shift_two).astype(jnp.bfloat16)
    hidden = matmul(inputs_two, w_up) + b_up
    active = jax.nn.gelu(hidden, approximate=True).astype(jnp.bfloat16)
    stream_out = stream_mid + matmul(active, w_down) + b_down
    saved_acts = (
        normed_one,
        scale_one,
        inputs_one,
        queries,
        key_rows,
        values,
        mixed_out,
        log_total,
        mixed_low,
        normed_two,
        scale_two,
        inputs_two,
        hidden,
        active,
    )
    return (stream_out, saved_acts)


def layer_back(grad_out, seg_own, first_place, gathered, saved_acts):
    (
        gain_one,
        shift_one,
        w_query,
        b_query,
        w_key,
        w_value,
        b_value,
        w_out,
        b_out,
        gain_two,
        shift_two,
        w_up,
        b_up,
        w_down,
        b_down,
    ) = gathered
    (
        normed_one,
        scale_one,
        inputs_one,
        queries,
        key_rows,
        values,
        mixed_out,
        log_total,
        mixed_low,
        normed_two,
        scale_two,
        inputs_two,
        hidden,
        active,
    ) = saved_acts
    width = w_query.shape[0]
    grad_branch = grad_out.astype(jnp.bfloat16)
    g_b_down = jnp.sum(grad_branch, axis=0, dtype=jnp.float32)
    g_w_down = contract_rows(active, grad_branch)
    grad_active = contract_cols(grad_branch, w_down)
    gelu_value, gelu_pull = jax.vjp(
        lambda inner_val: jax.nn.gelu(inner_val, approximate=True), hidden
    )
    grad_hidden = gelu_pull(grad_active)[0].astype(jnp.bfloat16)
    g_b_up = jnp.sum(grad_hidden, axis=0, dtype=jnp.float32)
    g_w_up = contract_rows(inputs_two, grad_hidden)
    grad_in_two = contract_cols(grad_hidden, w_up)
    g_gain_two = jnp.sum(grad_in_two * normed_two, axis=0)
    g_shift_two = jnp.sum(grad_in_two, axis=0)
    grad_mid = grad_out + norm_back(grad_in_two, normed_two, scale_two, gain_two)
    grad_attn = grad_mid.astype(jnp.bfloat16)
    g_b_out = jnp.sum(grad_attn, axis=0, dtype=jnp.float32)
    g_w_out = contract_rows(mixed_low, grad_attn)
    grad_mixed = contract_cols(grad_attn, w_out).astype(jnp.bfloat16)
    grad_q, grad_k, grad_v = attend_back(
        queries, mixed_out, grad_mixed, log_total, key_rows, values, seg_own, first_place
    )
    g_b_query = jnp.sum(grad_q, axis=0, dtype=jnp.float32)
    g_b_value = jnp.sum(grad_v, axis=0, dtype=jnp.float32)
    projected = jnp.concatenate([grad_q, grad_k, grad_v], axis=1)
    g_proj = contract_rows(inputs_one, projected)
    grad_in_one = (
        contract_cols(grad_q, w_query)
        + contract_cols(grad_k, w_key)
        + contract_cols(grad_v, w_value)
    )
    g_gain_one = jnp.sum(grad_in_one * normed_one, axis=0)
    g_shift_one = jnp.sum(grad_in_one, axis=0)
    grad_stream = grad_mid + norm_back(grad_in_one, normed_one, scale_one, gain_one)
    g_w_query = g_proj[:, 0:width]
    g_w_key = g_proj[:, width : 2 * width]
    g_w_value = g_proj[:, 2 * width :]
    return (
        grad_stream,
        (
            g_gain_one,
            g_shift_one,
            g_w_query,
            g_b_query,
            g_w_key,
            g_w_value,
            g_b_value,
            g_w_out,
            g_b_out,
            g_gain_two,
            g_shift_two,
            g_w_up,
            g_b_up,
            g_w_down,
            g_b_down,
        ),
    )


def send_all(terms):
    (
        t_gain_one,
        t_shift_one,
        t_w_query,
        t_b_query,
        t_w_key,
        t_w_value,
        t_b_value,
        t_w_out,
        t_b_out,
        t_gain_two,
        t_shift_two,
        t_w_up,
        t_b_up,
        t_w_down,
        t_b_down,
    ) = terms
    return (
        lax.psum_scatter(t_gain_one, ("dp", "ctx"), scatter_dimension=1, tiled=True),
        lax.psum_scatter(t_shift_one, ("dp", "ctx"), scatter_dimension=1, tiled=True),
        lax.psum_scatter(t_w_query, ("dp", "ctx"), scatter_dimension=1, tiled=True),
        lax.psum_scatter(t_b_query, ("dp", "ctx"), scatter_dimension=1, tiled=True),
        lax.psum_scatter(t_w_key, ("dp", "ctx"), scatter_dimension=1, tiled=True),
        lax.psum_scatter(t_w_value, ("dp", "ctx"), scatter_dimension=1, tiled=True),
        lax.psum_scatter(t_b_value, ("dp", "ctx"), scatter_dimension=1, tiled=True),
        lax.psum_scatter(t_w_out, ("dp", "ctx"), scatter_dimension=1, tiled=True),
        lax.psum_scatter(t_b_out, ("dp", "ctx"), scatter_dimension=1, tiled=True),
        lax.psum_scatter(t_gain_two, ("dp", "ctx"), scatter_dimension=1, tiled=True),
        lax.psum_scatter(t_shift_two, ("dp", "ctx"), scatter_dimension=1, tiled=True),
        lax.psum_scatter(t_w_up, ("dp", "ctx"), scatter_dimension=1, tiled=True),
        lax.psum_scatter(t_b_up, ("dp", "ctx"), scatter_dimension=1, tiled=True),
        lax.psum_scatter(t_w_down, ("dp", "ctx"), scatter_dimension=1, tiled=True),
        lax.psum_scatter(t_b_down, ("dp", "ctx"), scatter_dimension=1, tiled=True),
    )


def on_device(
    tokens,
    segments,
    ln1_gain,
    ln1_bias,
    w_query,
    b_query,
    w_key,
    w_value,
    b_value,
    w_out,
    b_out,
    ln2_gain,
    ln2_bias,
    w_up,
    b_up,
    w_down,
    b_down,
    out_grad,
):
    row_count = tokens.shape[1]
    layer_count = w_query.shape[0]
    first_place = lax.axis_index("ctx") * row_count
    seg_own = segments[0]
    every_layer = (
        lax.all_gather(ln1_gain, ("dp", "ctx"), axis=1, tiled=True),
        lax.all_gather(ln1_bias, ("dp", "ctx"), axis=1, tiled=True),
        lax.all_gather(w_query, ("dp", "ctx"), axis=1, tiled=True),
        lax.all_gather(b_query, ("dp", "ctx"), axis=1, tiled=True),
        lax.all_gather(w_key, ("dp", "ctx"), axis=1, tiled=True),
        lax.all_gather(w_value, ("dp", "ctx"), axis=1, tiled=True),
        lax.all_gather(b_value, ("dp", "ctx"), axis=1, tiled=True),
        lax.all_gather(w_out, ("dp", "ctx"), axis=1, tiled=True),
        lax.all_gather(b_out, ("dp", "ctx"), axis=1, tiled=True),
        lax.all_gather(ln2_gain, ("dp", "ctx"), axis=1, tiled=True),
        lax.all_gather(ln2_bias, ("dp", "ctx"), axis=1, tiled=True),
        lax.all_gather(w_up, ("dp", "ctx"), axis=1, tiled=True),
        lax.all_gather(b_up, ("dp", "ctx"), axis=1, tiled=True),
        lax.all_gather(w_down, ("dp", "ctx"), axis=1, tiled=True),
        lax.all_gather(b_down, ("dp", "ctx"), axis=1, tiled=True),
    )
    stream = tokens[0].astype(jnp.float32)
    kept_acts = []
    for layer_no in range(layer_count):
        gathered = tuple((member[layer_no] for member in every_layer))
        stream, saved_acts = layer_forward(stream, seg_own, first_place, gathered)
        kept_acts.append(saved_acts)
    output = stream.astype(jnp.bfloat16)[None]
    grad_stream = out_grad[0].astype(jnp.float32)
    collected = [None] * layer_count
    for layer_no in reversed(range(layer_count)):
        gathered = tuple((member[layer_no] for member in every_layer))
        grad_stream, terms = layer_back(
            grad_stream, seg_own, first_place, gathered, kept_acts[layer_no]
        )
        collected[layer_no] = terms
    stacked = tuple(
        (
            jnp.stack([collected[layer_no][index_no] for layer_no in range(layer_count)])
            for index_no in range(15)
        )
    )
    stacked = send_all(stacked)
    return (output, grad_stream[None]) + tuple(stacked)


def solution(mesh):
    in_specs = (
        P("dp", "ctx", None),
        P("dp", "ctx"),
        P(None, ("dp", "ctx")),
        P(None, ("dp", "ctx")),
        P(None, ("dp", "ctx"), None),
        P(None, ("dp", "ctx")),
        P(None, ("dp", "ctx"), None),
        P(None, ("dp", "ctx"), None),
        P(None, ("dp", "ctx")),
        P(None, ("dp", "ctx"), None),
        P(None, ("dp", "ctx")),
        P(None, ("dp", "ctx")),
        P(None, ("dp", "ctx")),
        P(None, ("dp", "ctx"), None),
        P(None, ("dp", "ctx")),
        P(None, ("dp", "ctx"), None),
        P(None, ("dp", "ctx")),
        P("dp", "ctx", None),
    )
    out_specs = (
        P("dp", "ctx", None),
        P("dp", "ctx", None),
        P(None, ("dp", "ctx")),
        P(None, ("dp", "ctx")),
        P(None, ("dp", "ctx"), None),
        P(None, ("dp", "ctx")),
        P(None, ("dp", "ctx"), None),
        P(None, ("dp", "ctx"), None),
        P(None, ("dp", "ctx")),
        P(None, ("dp", "ctx"), None),
        P(None, ("dp", "ctx")),
        P(None, ("dp", "ctx")),
        P(None, ("dp", "ctx")),
        P(None, ("dp", "ctx"), None),
        P(None, ("dp", "ctx")),
        P(None, ("dp", "ctx"), None),
        P(None, ("dp", "ctx")),
    )
    return jax.shard_map(
        on_device, mesh=mesh, in_specs=in_specs, out_specs=out_specs, check_vma=False
    )
```

profile of v0, /device:TPU:0, one launch (start us, length us, event | category | flops | bytes accessed | tf_op | source)
XLA Modules:
  0.0 1684.6 jit_solution(8009425502608613152)
XLA Ops:
  9.5 43.2 %all-gather.2 = bf16[32,24,2]{1,2,0:T(2,128)(2,1)S(1)} all-gather(bf16[1,24,2]{1,2,0:T(2,128)(2,1)} %bitcast.542), channel_id=1, replica_groups=mesh['dp'=8,'ctx'=4] {'dp','ctx'}, dimensions={0}, use_global_device_ids=true | all-gather | bytes 3168 | tf_op jit(solution)/shard_map/all_gather | solution.py:448
  52.8 36.6 %all-gather.1 = bf16[32,24,2]{1,2,0:T(2,128)(2,1)S(1)} all-gather(bf16[1,24,2]{1,2,0:T(2,128)(2,1)} %bitcast.543), channel_id=1, replica_groups=mesh['dp'=8,'ctx'=4] {'dp','ctx'}, dimensions={0}, use_global_device_ids=true | all-gather | bytes 3168 | tf_op jit(solution)/shard_map/all_gather | solution.py:447
  94.8 37.9 %all-gather.4 = bf16[32,24,2]{1,2,0:T(2,128)(2,1)S(1)} all-gather(bf16[1,24,2]{1,2,0:T(2,128)(2,1)S(1)} %bitcast.544), channel_id=1, replica_groups=mesh['dp'=8,'ctx'=4] {'dp','ctx'}, dimensions={0}, use_global_device_ids=true | all-gather | bytes 3168 | tf_op jit(solution)/shard_map/all_gather | solution.py:453
  138.2 36.5 %all-gather.5 = bf16[32,24,2]{1,2,0:T(2,128)(2,1)S(1)} all-gather(bf16[1,24,2]{1,2,0:T(2,128)(2,1)S(1)} %bitcast.545), channel_id=1, replica_groups=mesh['dp'=8,'ctx'=4] {'dp','ctx'}, dimensions={0}, use_global_device_ids=true | all-gather | bytes 3168 | tf_op jit(solution)/shard_map/all_gather | solution.py:455
  174.8 37.8 %all-gather.9 = bf16[32,24,2]{1,2,0:T(2,128)(2,1)S(1)} all-gather(bf16[1,24,2]{1,2,0:T(2,128)(2,1)S(1)} %bitcast.546), channel_id=1, replica_groups=mesh['dp'=8,'ctx'=4] {'dp','ctx'}, dimensions={0}, use_global_device_ids=true | all-gather | bytes 3168 | tf_op jit(solution)/shard_map/all_gather | solution.py:461
  220.2 36.4 %all-gather.3 = bf16[32,24,2]{1,2,0:T(2,128)(2,1)S(1)} all-gather(bf16[1,24,2]{1,2,0:T(2,128)(2,1)S(1)} %bitcast.547), channel_id=1, replica_groups=mesh['dp'=8,'ctx'=4] {'dp','ctx'}, dimensions={0}, use_global_device_ids=true | all-gather | bytes 3168 | tf_op jit(solution)/shard_map/all_gather | solution.py:450
  256.8 37.8 %all-gather.8 = bf16[32,96,2]{1,2,0:T(2,128)(2,1)S(1)} all-gather(bf16[1,96,2]{1,2,0:T(2,128)(2,1)S(1)} %bitcast.548), channel_id=1, replica_groups=mesh['dp'=8,'ctx'=4] {'dp','ctx'}, dimensions={0}, use_global_device_ids=true | all-gather | bytes 12672 | tf_op jit(solution)/shard_map/all_gather | solution.py:459
  294.8 36.5 %all-gather.7 = bf16[32,24,2]{1,2,0:T(2,128)(2,1)S(1)} all-gather(bf16[1,24,2]{1,2,0:T(2,128)(2,1)S(1)} %bitcast.549), channel_id=1, replica_groups=mesh['dp'=8,'ctx'=4] {'dp','ctx'}, dimensions={0}, use_global_device_ids=true | all-gather | bytes 3168 | tf_op jit(solution)/shard_map/all_gather | solution.py:457
  331.4 38.1 %all-gather.6 = bf16[32,24,2]{1,2,0:T(2,128)(2,1)S(1)} all-gather(bf16[1,24,2]{1,2,0:T(2,128)(2,1)S(1)} %bitcast.550), channel_id=1, replica_groups=mesh['dp'=8,'ctx'=4] {'dp','ctx'}, dimensions={0}, use_global_device_ids=true | all-gather | bytes 3168 | tf_op jit(solution)/shard_map/all_gather | solution.py:456
  376.9 22.0 %conditional.6 = (f32[12,256]{1,0:T(8,128)}, f32[12,256]{1,0:T(8,128)}, f32[256,12,64]{0,2,1:T(8,128)S(1)}, f32[12,256]{1,0:T(8,128)S(1)}) conditional(s32[]{:T(128)} %convert_element_type.348, () %tuple.128, (s32[256]{0:T(256)}, f32[1024]{0:T(1024)}, f32[256]{0:T(256)S(1)}, bf16[1024,768]{1,0:T(8,128)(2,1)}, bf16[256,12,64]{0,2,1:T(8,128)(2,1)}, ...), branch_computations={%region_2.0_spmd, %region_3.6_spmd} | conditional | flops 846984192 | bytes 106141784 | solution.py:91
  407.8 51.4 %all-gather.39.cloned.1.call-done = bf16[2,3072,768]{2,1,0:T(8,128)(2,1)} async-done(((bf16[2,96,768]{2,1,0:T(8,128)(2,1)}), bf16[2,3072,768]{2,1,0:T(8,128)(2,1)}) %all-gather.39.cloned.1.call-update) | async-done | bytes 9437200 | tf_op jit(solution)/shard_map/all_gather | solution.py:460
  485.4 21.1 %all-gather.43.cloned.1.call-done = bf16[1024,768]{1,0:T(8,128)(2,1)} async-done(((bf16[256,768]{1,0:T(8,128)(2,1)}), bf16[1024,768]{1,0:T(8,128)(2,1)}) %all-gather.43.cloned.1.call-update) | async-done | bytes 1572880 | tf_op jit(solution)/shard_map/all_gather | solution.py:60
  506.5 20.3 %conditional.7 = (f32[12,256]{1,0:T(8,128)S(1)}, f32[12,256]{1,0:T(8,128)}, f32[256,12,64]{0,2,1:T(8,128)S(1)}, f32[12,256]{1,0:T(8,128)S(1)}) conditional(s32[]{:T(128)} %convert_element_type.348, () %tuple.130, (s32[256]{0:T(256)}, f32[1024]{0:T(1024)}, f32[256]{0:T(256)S(1)}, bf16[1024,768]{1,0:T(8,128)(2,1)}, ...), branch_computations={%region_10.11_spmd, %region_11.14_spmd} | conditional | flops 846984192 | bytes 107288744 | solution.py:91
  565.4 21.7 %while.64 = (s32[]{:T(128)}, f32[256,12,64]{0,2,1:T(8,128)}, s32[2]{0:T(128)}, s32[]{:T(128)}, bf16[2,512]{1,0:T(2,128)(2,1)S(1)}, /*index=5*/f32[]{:T(128)}, f3...) while((s32[]{:T(128)}, f32[256,12,64]{0,2,1:T(8,128)}, ...), condition=%wide.region_22.23_spmd.clone, body=%wide.region_19.22_spmd.clone.sunk | while | flops 615777536 | bytes 20752736 | solution.py:163
  616.7 49.1 %while.66 = (s32[]{:T(128)}, f32[256,12,64]{0,2,1:T(8,128)S(1)}, f32[256,12,64]{0,2,1:T(8,128)}, s32[2]{0:T(128)}, s32[]{:T(128)}, /*index=5*/bf16[2,512]{1,0:T(...) while((s32[]{:T(128)}, f32[256,12,64]{0,2,1:T(8,128)S(1)}, ...), condition=%wide.region_26.27_spmd.clone.clone, body=%wide.region_23.26_spmd.clone.clone.sunk | while | flops 825165056 | bytes 36366864 | solution.py:232
  720.1 22.1 %while.65 = (s32[]{:T(128)}, f32[256,12,64]{0,2,1:T(8,128)}, s32[2]{0:T(128)}, s32[]{:T(128)}, bf16[2,512]{1,0:T(2,128)(2,1)S(1)}, /*index=5*/f32[]{:T(128)}, f3...) while((s32[]{:T(128)}, f32[256,12,64]{0,2,1:T(8,128)}, ...), condition=%wide.region_35.36_spmd.clone, body=%wide.region_32.35_spmd.clone.sunk | while | flops 615777536 | bytes 20748612 | solution.py:163
  754.0 49.2 %while.67 = (s32[]{:T(128)}, f32[256,12,64]{0,2,1:T(8,128)S(1)}, f32[256,12,64]{0,2,1:T(8,128)}, s32[2]{0:T(128)}, s32[]{:T(128)}, /*index=5*/bf16[2,512]{1,0:T(...) while((s32[]{:T(128)}, f32[256,12,64]{0,2,1:T(8,128)S(1)}, ...), condition=%wide.region_39.40_spmd.clone.clone, body=%wide.region_36.39_spmd.clone.clone.sunk | while | flops 825165056 | bytes 36366864 | solution.py:232
  758.3 20.2 %conditional.21 = ((f32[256,12,64]{0,2,1:T(8,128)S(1)}, f32[256,12,64]{0,2,1:T(8,128)})) conditional(s32[]{:T(128)} %convert_element_type.615, (f32[256,12,64]{0,2,1:T(8,128)S(1)}, f32[256,12,64]{0,2,1:T(8,128)}) %tuple.279, (s32[]{:T(128)}, s32[]{:T(128)}, f32[256]{0:T(256)S(1)}, f32[1,512]{1,0:T(1,128)S(1)}, bf16[2,512,768]{1,2,0:T(8,128)(2,1)S(1)}, ...), branch_computations={%region_37.37_spmd, %region_38.38_spmd} | conditional | flops 825164544 | bytes 36362420 | solution.py:229
  866.5 40.6 %all-reduce.8 = (f32[2,768]{1,0:T(2,128)S(1)}, f32[2,768]{1,0:T(2,128)S(1)}, f32[2,768]{1,0:T(2,128)S(1)}, f32[2,768]{1,0:T(2,128)S(1)}, f32[2,768]{1,0:T(2,128)...) all-reduce(f32[2,768]{1,0:T(2,128)S(1)} %pad_maximum_fusion.7, ...), channel_id=3, replica_groups=mesh['dp'=8,'ctx'=4] {'dp','ctx'}, use_global_device_ids=true, to_apply=%region_44.45.clone | all-reduce | flops 12288 | bytes 98304
  917.3 112.9 %reduce-scatter.18.cloned.1.call-done = f32[2,24,768]{2,1,0:T(8,128)} async-done(((f32[2,768,768]{2,1,0:T(8,128)}), f32[2,24,768]{2,1,0:T(8,128)}) %reduce-scatter.18.cloned.1.call-update) | async-done | bytes 147472 | tf_op jit(solution)/shard_map/reduce_scatter | solution.py:406
  1030.2 112.0 %reduce-scatter.20.cloned.1.call-done = f32[2,24,768]{2,1,0:T(8,128)} async-done(((f32[2,768,768]{2,1,0:T(8,128)}), f32[2,24,768]{2,1,0:T(8,128)}) %reduce-scatter.20.cloned.1.call-update) | async-done | bytes 147472 | tf_op jit(solution)/shard_map/reduce_scatter | solution.py:408
  1142.3 113.1 %reduce-scatter.22.cloned.1.call-done = f32[2,24,768]{2,1,0:T(8,128)} async-done(((f32[2,768,768]{2,1,0:T(8,128)}), f32[2,24,768]{2,1,0:T(8,128)}) %reduce-scatter.22.cloned.1.call-update) | async-done | bytes 147472 | tf_op jit(solution)/shard_map/reduce_scatter | solution.py:409
  1255.4 211.0 %reduce-scatter.26.cloned.1.call-done = f32[2,24,3072]{2,1,0:T(8,128)} async-done(((f32[2,768,3072]{2,1,0:T(8,128)}), f32[2,24,3072]{2,1,0:T(8,128)}) %reduce-scatter.26.cloned.1.call-update) | async-done | bytes 589840 | tf_op jit(solution)/shard_map/reduce_scatter | solution.py:415
  1466.4 211.1 %reduce-scatter.28.cloned.1.call-done = f32[2,96,768]{2,1,0:T(8,128)} async-done(((f32[2,3072,768]{2,1,0:T(8,128)}), f32[2,96,768]{2,1,0:T(8,128)}) %reduce-scatter.28.cloned.1.call-update) | async-done | bytes 589840 | tf_op jit(solution)/shard_map/reduce_scatter | solution.py:417
  (638 shorter events, 522.9 us)
Async XLA Ops:
  7.2 84.8 %all-gather.25.cloned.1.call-start = ((), (), s32[]{:S(2)}) async-start(), calls=%async_computation.7 | async-start | bytes 2433024 | tf_op jit(solution)/shard_map/all_gather | solution.py:451
  7.9 125.5 %all-gather.31.cloned.1.call-start = ((), (), s32[]{:S(2)}) async-start(), calls=%async_computation.10 | async-start | bytes 2433024 | tf_op jit(solution)/shard_map/all_gather | solution.py:452
  8.7 365.2 %all-gather.29.cloned.1.call-start = ((), (), s32[]{:S(2)}) async-start(), calls=%async_computation.9 | async-start | bytes 2433024 | tf_op jit(solution)/shard_map/all_gather | solution.py:449
  9.4 367.4 %all-gather.27.cloned.1.call-start = ((), (), s32[]{:S(2)}) async-start(), calls=%async_computation.8 | async-start | bytes 1966080 | tf_op jit(solution)/shard_map/all_gather | solution.py:59
  89.5 284.4 %copy-start.65 = (f32[768]{0:T(1024)}, f32[768]{0:T(1024)S(1)}, u32[]{:S(2)}) copy-start(f32[768]{0:T(1024)S(1)} %get-tuple-element.1896) | copy-start | bytes 9220
  89.6 284.4 %copy-start.76 = (f32[768]{0:T(1024)}, f32[768]{0:T(1024)S(1)}, u32[]{:S(2)}) copy-start(f32[768]{0:T(1024)S(1)} %get-tuple-element.1718) | copy-start | bytes 9220
  90.7 283.2 %copy-start.93 = (f32[256]{0:T(256)}, f32[256]{0:T(256)S(1)}, u32[]{:S(2)}) copy-start(f32[256]{0:T(256)S(1)} %broadcast_multiply_fusion.11) | copy-start | bytes 3076
  94.8 282.1 %all-gather.33.cloned.1.call-start = ((), (), s32[]{:S(2)}) async-start(), calls=%async_computation.11 | async-start | bytes 1966080 | tf_op jit(solution)/shard_map/all_gather | solution.py:60
  136.1 263.7 %all-gather.35.cloned.1.call-start = ((), (), s32[]{:S(2)}) async-start(), calls=%async_computation.12 | async-start | bytes 2433024 | tf_op jit(solution)/shard_map/all_gather | solution.py:454
  136.7 265.4 %all-gather.37.cloned.1.call-start = ((), (), s32[]{:S(2)}) async-start(), calls=%async_computation.13 | async-start | bytes 9732096 | tf_op jit(solution)/shard_map/all_gather | solution.py:458
  137.4 321.8 %all-gather.39.cloned.1.call-start = ((), (), s32[]{:S(2)}) async-start(), calls=%async_computation.14 | async-start | bytes 9732096 | tf_op jit(solution)/shard_map/all_gather | solution.py:460
  138.2 347.2 %all-gather.41.cloned.1.call-start = ((), (), s32[]{:S(2)}) async-start(), calls=%async_computation.15 | async-start | bytes 1966080 | tf_op jit(solution)/shard_map/all_gather | solution.py:59
  467.0 39.5 %all-gather.43.cloned.1.call-start = ((), (), s32[]{:S(2)}) async-start(), calls=%async_computation.16 | async-start | bytes 1966080 | tf_op jit(solution)/shard_map/all_gather | solution.py:60
  469.6 119.5 %all-gather.45.cloned.1.call-start = ((), (), s32[]{:S(2)}) async-start(), calls=%async_computation.17 | async-start | bytes 1966080 | tf_op jit(solution)/shard_map/all_gather | solution.py:167
  472.8 140.2 %all-gather.47.cloned.1.call-start = ((), (), s32[]{:S(2)}) async-start(), calls=%async_computation.18 | async-start | bytes 1966080 | tf_op jit(solution)/shard_map/all_gather | solution.py:168
  546.6 154.8 %all-gather.49.cloned.1.call-start = ((), (), s32[]{:S(2)}) async-start(), calls=%async_computation.19 | async-start | bytes 1966080 | tf_op jit(solution)/shard_map/all_gather | solution.py:167
  547.3 203.0 %all-gather.51.cloned.1.call-start = ((), (), s32[]{:S(2)}) async-start(), calls=%async_computation.20 | async-start | bytes 1966080 | tf_op jit(solution)/shard_map/all_gather | solution.py:168
  683.3 177.6 %reduce-scatter.30.cloned.1.call-start = ((), (), s32[]{:S(2)}) async-start(), calls=%async_computation.27 | async-start | bytes 1622016
  690.4 226.9 %reduce-scatter.24.cloned.1.call-start = ((), (), s32[]{:S(2)}) async-start(), calls=%async_computation.24 | async-start | bytes 4866048 | tf_op jit(solution)/shard_map/reduce_scatter | solution.py:411
  694.8 335.4 %reduce-scatter.18.cloned.1.call-start = ((), (), s32[]{:S(2)}) async-start(), calls=%async_computation.21 | async-start | bytes 4866048 | tf_op jit(solution)/shard_map/reduce_scatter | solution.py:406
  812.2 330.0 %reduce-scatter.20.cloned.1.call-start = ((), (), s32[]{:S(2)}) async-start(), calls=%async_computation.22 | async-start | bytes 4866048 | tf_op jit(solution)/shard_map/reduce_scatter | solution.py:408
  818.0 437.4 %reduce-scatter.22.cloned.1.call-start = ((), (), s32[]{:S(2)}) async-start(), calls=%async_computation.23 | async-start | bytes 4866048 | tf_op jit(solution)/shard_map/reduce_scatter | solution.py:409
  823.9 642.5 %reduce-scatter.26.cloned.1.call-start = ((), (), s32[]{:S(2)}) async-start(), calls=%async_computation.25 | async-start | bytes 19464192 | tf_op jit(solution)/shard_map/reduce_scatter | solution.py:415
  836.9 840.6 %reduce-scatter.28.cloned.1.call-start = ((), (), s32[]{:S(2)}) async-start(), calls=%async_computation.26 | async-start | bytes 19464192 | tf_op jit(solution)/shard_map/reduce_scatter | solution.py:417
  (147 other events, 2715.8 us)
Sparse Core Ops, SparseCore 0:
  11.0 60.0 all-gather.24
  74.0 56.1 all-gather.30
  133.2 56.0 all-gather.28
  191.3 18.5 all-gather.26
  211.9 19.6 all-gather.32
  234.4 57.2 all-gather.34
  294.7 80.9 all-gather.36
  378.6 80.5 all-gather.38
  467.1 18.2 all-gather.40
  486.8 19.6 all-gather.42
  508.1 19.6 all-gather.44
  546.7 20.0 all-gather.46
  568.4 19.6 all-gather.48
  683.4 19.6 all-gather.50
  708.3 96.9 reduce-scatter.29
  811.2 106.0 reduce-scatter.23
  924.1 106.0 reduce-scatter.17
  1036.1 106.1 reduce-scatter.19
  1149.2 106.1 reduce-scatter.21
  1262.2 204.1 reduce-scatter.25
  1473.4 204.0 reduce-scatter.27
where the time goes:
time: 1690 us; the launch traced here: 1680 us
  waiting for transfers between devices  854 us (51%)
  blocking collectives  422 us (25%)
  matrix products  194 us (11%)
  local copies, waits for them, and re-layouts  99.7 us (6%)
  other arithmetic  79.4 us (5%)
  between operations  17.7 us (1%)
  loops' own time  17.5 us (1%)
    reduce_scatter x1, waiting for transfers between devices, send_all(): lax.psum_scatter(t_w_down, ('dp', 'ctx'), scatter_dimension=1, tiled=True)  211 us
    reduce_scatter x1, waiting for transfers between devices, send_all(): lax.psum_scatter(t_w_up, ('dp', 'ctx'), scatter_dimension=1, tiled=True)  211 us
    reduce_scatter x1, waiting for transfers between devices, send_all(): lax.psum_scatter(t_w_value, ('dp', 'ctx'), scatter_dimension=1, tiled=True)  113 us
    reduce_scatter x1, waiting for transfers between devices, send_all(): lax.psum_scatter(t_w_query, ('dp', 'ctx'), scatter_dimension=1, tiled=True)  113 us
    reduce_scatter x1, waiting for transfers between devices, send_all(): lax.psum_scatter(t_w_key, ('dp', 'ctx'), scatter_dimension=1, tiled=True)  112 us
    all_gather x1, waiting for transfers between devices, on_device(): lax.all_gather(w_down, ('dp', 'ctx'), axis=1, tiled=True)  51.4 us
    all_gather x1, blocking collectives, on_device(): lax.all_gather(ln1_bias, ('dp', 'ctx'), axis=1, tiled=True)  43.2 us
    unnamed x1, blocking collectives  40.6 us
  transfers between devices with their start and end apart: 21, of which 9 were waited for; matrix products, arithmetic and copies ran while one was open for 21% of the time, Pallas kernels for 0%

commit v1 on v0

v1 whole, which is shorter than its diff:
```python
import jax
import jax.numpy as jnp
from jax import lax
from jax.sharding import PartitionSpec as P

H = 12
HD = 64


EPSILON = 1e-05
MASKED = -1e30


def matmul(left_op, right_op):
    return jnp.dot(left_op, right_op, preferred_element_type=jnp.float32)


def contract_rows(left_op, right_op):
    return lax.dot_general(
        left_op, right_op, (((0,), (0,)), ((), ())), preferred_element_type=jnp.float32
    )


def contract_cols(left_op, right_op):
    return lax.dot_general(
        left_op, right_op, (((1,), (1,)), ((), ())), preferred_element_type=jnp.float32
    )


def normalize(values):
    centre = jnp.mean(values, axis=-1, keepdims=True)
    centred = values - centre
    scale_vec = lax.rsqrt(jnp.mean(centred * centred, axis=-1, keepdims=True) + EPSILON)
    return (centred * scale_vec, scale_vec)


def norm_back(grad_in, normed, scale_vec, gain_vec):
    scaled = grad_in * gain_vec
    return scale_vec * (
        scaled
        - jnp.mean(scaled, axis=-1, keepdims=True)
        - normed * jnp.mean(scaled * normed, axis=-1, keepdims=True)
    )


def to_heads(blocks_in, parts):
    shards = lax.axis_size("ctx")
    row_count = blocks_in[0].shape[0]
    per = -(-H // shards)
    spare = (per * shards - H) * HD
    sent = jnp.stack([jnp.pad(b, ((0, 0), (0, spare))) for b in blocks_in])
    sent = sent.reshape(parts, row_count, shards, per * HD).transpose(2, 0, 1, 3)
    got = lax.all_to_all(sent, "ctx", 0, 0, tiled=True)
    got = got.reshape(shards, parts, row_count, per, HD).transpose(1, 3, 0, 2, 4)
    return got.reshape(parts, per, shards * row_count, HD)


def from_heads(heads_in):
    shards = lax.axis_size("ctx")
    parts, per, seq_len = heads_in.shape[:3]
    row_count = seq_len // shards
    sent = heads_in.reshape(parts, per, shards, row_count, HD).transpose(2, 0, 3, 1, 4)
    sent = sent.reshape(shards, parts, row_count, per * HD)
    got = lax.all_to_all(sent, "ctx", 0, 0, tiled=True)
    got = got.transpose(1, 2, 0, 3).reshape(parts, row_count, shards * per * HD)
    return got[:, :, : H * HD]


def head_dot(left_op, right_op, left_dim, right_dim):
    return lax.dot_general(
        left_op,
        right_op,
        (((left_dim,), (right_dim,)), ((0,), (0,))),
        preferred_element_type=jnp.float32,
    )


def attend_forward(heads, allowed):
    queries, key_rows, values = heads[0], heads[1], heads[2]
    scores = head_dot(queries, key_rows, 2, 2) * HD ** (-0.5)
    scores = jnp.where(allowed[None], scores, MASKED)
    highest = jnp.max(scores, axis=-1, keepdims=True)
    weights = jnp.exp(scores - highest)
    totals = jnp.sum(weights, axis=-1, keepdims=True)
    mixed_out = head_dot(weights.astype(jnp.bfloat16), values, 2, 1) / totals
    return (mixed_out, highest + jnp.log(totals))


def attend_back(heads, mixed_out, grad_mixed, log_total, allowed):
    queries, key_rows, values = heads[0], heads[1], heads[2]
    score_scale = HD ** (-0.5)
    row_delta = jnp.sum(grad_mixed.astype(jnp.float32) * mixed_out, axis=-1, keepdims=True)
    scores = head_dot(queries, key_rows, 2, 2) * score_scale
    probs = jnp.exp(jnp.where(allowed[None], scores, MASKED) - log_total)
    grad_p = head_dot(grad_mixed, values, 2, 2)
    grad_s = (probs * (grad_p - row_delta)).astype(jnp.bfloat16)
    grad_q = head_dot(grad_s, key_rows, 2, 1) * score_scale
    grad_k = head_dot(grad_s, queries, 1, 1) * score_scale
    grad_v = head_dot(probs.astype(jnp.bfloat16), grad_mixed, 1, 1)
    return jnp.stack([grad_q, grad_k, grad_v]).astype(jnp.bfloat16)


def layer_forward(stream, allowed, gathered):
    w_qkv, w_out, w_up, w_down, vectors = gathered
    gain_one, shift_one, b_query, b_value, b_out, gain_two, shift_two, b_down, b_up = vectors
    width = w_out.shape[1]
    normed_one, scale_one = normalize(stream)
    inputs_one = (normed_one * gain_one + shift_one).astype(jnp.bfloat16)
    bias_all = jnp.concatenate([b_query, jnp.zeros_like(b_query), b_value])
    projected = (matmul(inputs_one, w_qkv) + bias_all).astype(jnp.bfloat16)
    heads = to_heads([projected[:, p * width : (p + 1) * width] for p in range(3)], 3)
    mixed_out, log_total = attend_forward(heads, allowed)
    mixed_low = from_heads(mixed_out.astype(jnp.bfloat16)[None])[0]
    stream_mid = stream + matmul(mixed_low, w_out) + b_out
    normed_two, scale_two = normalize(stream_mid)
    inputs_two = (normed_two * gain_two + shift_two).astype(jnp.bfloat16)
    hidden = matmul(inputs_two, w_up) + b_up
    active = jax.nn.gelu(hidden, approximate=True).astype(jnp.bfloat16)
    stream_out = stream_mid + matmul(active, w_down) + b_down
    saved_acts = (
        normed_one,
        scale_one,
        inputs_one,
        heads,
        mixed_out,
        log_total,
        mixed_low,
        normed_two,
        scale_two,
        inputs_two,
        hidden,
        active,
    )
    return (stream_out, saved_acts)


def column_sums(values):
    return jnp.sum(values, axis=0, dtype=jnp.float32)


def layer_back(grad_out, allowed, gathered, saved_acts):
    w_qkv, w_out, w_up, w_down, vectors = gathered
    gain_one, shift_one, b_query, b_value, b_out, gain_two, shift_two, b_down, b_up = vectors
    (
        normed_one,
        scale_one,
        inputs_one,
        heads,
        mixed_out,
        log_total,
        mixed_low,
        normed_two,
        scale_two,
        inputs_two,
        hidden,
        active,
    ) = saved_acts
    width = w_out.shape[1]
    grad_branch = grad_out.astype(jnp.bfloat16)
    g_b_down = column_sums(grad_branch)
    g_w_down = contract_rows(active, grad_branch)
    grad_active = contract_cols(grad_branch, w_down)
    gelu_value, gelu_pull = jax.vjp(
        lambda inner_val: jax.nn.gelu(inner_val, approximate=True), hidden
    )
    grad_hidden = gelu_pull(grad_active)[0].astype(jnp.bfloat16)
    g_b_up = column_sums(grad_hidden)
    g_w_up = contract_rows(inputs_two, grad_hidden)
    grad_in_two = contract_cols(grad_hidden, w_up)
    g_gain_two = jnp.sum(grad_in_two * normed_two, axis=0)
    g_shift_two = jnp.sum(grad_in_two, axis=0)
    grad_mid = grad_out + norm_back(grad_in_two, normed_two, scale_two, gain_two)
    grad_attn = grad_mid.astype(jnp.bfloat16)
    g_b_out = column_sums(grad_attn)
    g_w_out = contract_rows(mixed_low, grad_attn)
    grad_mixed = contract_cols(grad_attn, w_out).astype(jnp.bfloat16)
    grad_heads = attend_back(
        heads, mixed_out, to_heads([grad_mixed], 1)[0], log_total, allowed
    )
    back = from_heads(grad_heads)
    projected = jnp.concatenate([back[0], back[1], back[2]], axis=1)
    g_bias = column_sums(projected)
    g_proj = contract_rows(inputs_one, projected)
    grad_in_one = contract_cols(projected, w_qkv)
    g_gain_one = jnp.sum(grad_in_one * normed_one, axis=0)
    g_shift_one = jnp.sum(grad_in_one, axis=0)
    grad_stream = grad_mid + norm_back(grad_in_one, normed_one, scale_one, gain_one)
    g_vectors = (
        g_gain_one,
        g_shift_one,
        g_bias[:width],
        g_bias[2 * width :],
        g_b_out,
        g_gain_two,
        g_shift_two,
        g_b_down,
        g_b_up,
    )
    return (grad_stream, (g_proj, g_w_out, g_w_up, g_w_down, g_vectors))


def column_pieces(matrix, width):
    return [matrix[..., c : c + width] for c in range(0, matrix.shape[-1], width)]


def pad_rows(packed):
    rows = packed.shape[-2]
    return jnp.pad(packed, ((0, 0),) * (packed.ndim - 2) + ((0, -rows % 16), (0, 0)))


def pack_vectors(vectors, width):
    joined = jnp.concatenate(vectors, axis=-1)
    short = -joined.shape[-1] % width
    joined = jnp.pad(joined, ((0, 0),) * (joined.ndim - 1) + ((0, short),))
    return joined.reshape(joined.shape[:-1] + (-1, width))


def gather_layer(matrices, vectors):
    w_query, w_key, w_value, w_out, w_up, w_down = matrices
    rows, width = w_query.shape
    up_count = w_up.shape[1] // width
    pieces = [w_query, w_key, w_value, w_out] + column_pieces(w_up, width)
    packed = jnp.concatenate(pieces + [w_down, pack_vectors(vectors, width)], axis=0)
    whole = lax.all_gather(pad_rows(packed), ("dp", "ctx"), axis=0, tiled=False)

    def taken(first, count):
        return whole[:, first : first + count].reshape(-1, width)

    parts = [taken(i * rows, rows) for i in range(4 + up_count)]
    start = (4 + up_count) * rows
    down = taken(start, w_down.shape[0])
    start += w_down.shape[0]
    flat = whole[:, start:].reshape(whole.shape[0], -1)
    out_vectors = []
    place = 0
    for vector in vectors:
        out_vectors.append(flat[:, place : place + vector.shape[0]].reshape(-1))
        place += vector.shape[0]
    return (
        jnp.concatenate(parts[:3], axis=1),
        parts[3],
        jnp.concatenate(parts[4:], axis=1),
        down,
        tuple(out_vectors),
    )


def scatter_layer(terms):
    g_proj, g_w_out, g_w_up, g_w_down, g_vectors = terms
    width = g_w_out.shape[1]
    shards = lax.axis_size(("dp", "ctx"))
    blocks = column_pieces(g_proj, width) + [g_w_out] + column_pieces(g_w_up, width) + [g_w_down]
    blocks = [b.astype(jnp.bfloat16).reshape(shards, -1, width) for b in blocks]
    rows, down_rows = blocks[0].shape[1], blocks[-1].shape[1]
    vectors = [v.astype(jnp.bfloat16).reshape(shards, -1) for v in g_vectors]
    packed = jnp.concatenate(blocks + [pack_vectors(vectors, width)], axis=1)
    own = lax.psum_scatter(
        pad_rows(packed), ("dp", "ctx"), scatter_dimension=0, tiled=False
    ).astype(jnp.float32)
    up_count = len(blocks) - 5
    parts = [own[i * rows : (i + 1) * rows] for i in range(4 + up_count)]
    start = (4 + up_count) * rows
    down = own[start : start + down_rows]
    flat = own[start + down_rows :].reshape(-1)
    out_vectors = []
    place = 0
    for vector in vectors:
        out_vectors.append(flat[place : place + vector.shape[1]])
        place += vector.shape[1]
    gain_one, shift_one, b_query, b_value, b_out, gain_two, shift_two, b_down, b_up = out_vectors
    return (
        gain_one,
        shift_one,
        parts[0],
        b_query,
        parts[1],
        parts[2],
        b_value,
        parts[3],
        b_out,
        gain_two,
        shift_two,
        jnp.concatenate(parts[4:], axis=1),
        b_up,
        down,
        b_down,
    )


def on_device(
    tokens,
    segments,
    ln1_gain,
    ln1_bias,
    w_query,
    b_query,
    w_key,
    w_value,
    b_value,
    w_out,
    b_out,
    ln2_gain,
    ln2_bias,
    w_up,
    b_up,
    w_down,
    b_down,
    out_grad,
):
    layer_count = w_query.shape[0]
    seg_all = lax.all_gather(segments[0].astype(jnp.bfloat16), "ctx", axis=0, tiled=True)
    seg_all = seg_all.astype(jnp.float32)
    place = jnp.arange(seg_all.shape[0])
    allowed = (place[None, :] <= place[:, None]) & (seg_all[None, :] == seg_all[:, None])
    matrices = (w_query, w_key, w_value, w_out, w_up, w_down)
    vectors = (ln1_gain, ln1_bias, b_query, b_value, b_out, ln2_gain, ln2_bias, b_down, b_up)
    every_layer = [
        gather_layer([m[l] for m in matrices], [v[l] for v in vectors])
        for l in range(layer_count)
    ]
    stream = tokens[0].astype(jnp.float32)
    kept_acts = []
    for layer_no in range(layer_count):
        stream, saved_acts = layer_forward(stream, allowed, every_layer[layer_no])
        kept_acts.append(saved_acts)
    output = stream.astype(jnp.bfloat16)[None]
    grad_stream = out_grad[0].astype(jnp.float32)
    collected = [None] * layer_count
    for layer_no in reversed(range(layer_count)):
        grad_stream, terms = layer_back(
            grad_stream, allowed, every_layer[layer_no], kept_acts[layer_no]
        )
        collected[layer_no] = scatter_layer(terms)
    stacked = tuple(jnp.stack(members) for members in zip(*collected))
    return (output, grad_stream[None]) + stacked


def solution(mesh):
    in_specs = (
        P("dp", "ctx", None),
        P("dp", "ctx"),
        P(None, ("dp", "ctx")),
        P(None, ("dp", "ctx")),
        P(None, ("dp", "ctx"), None),
        P(None, ("dp", "ctx")),
        P(None, ("dp", "ctx"), None),
        P(None, ("dp", "ctx"), None),
        P(None, ("dp", "ctx")),
        P(None, ("dp", "ctx"), None),
        P(None, ("dp", "ctx")),
        P(None, ("dp", "ctx")),
        P(None, ("dp", "ctx")),
        P(None, ("dp", "ctx"), None),
        P(None, ("dp", "ctx")),
        P(None, ("dp", "ctx"), None),
        P(None, ("dp", "ctx")),
        P("dp", "ctx", None),
    )
    out_specs = (
        P("dp", "ctx", None),
        P("dp", "ctx", None),
        P(None, ("dp", "ctx")),
        P(None, ("dp", "ctx")),
        P(None, ("dp", "ctx"), None),
        P(None, ("dp", "ctx")),
        P(None, ("dp", "ctx"), None),
        P(None, ("dp", "ctx"), None),
        P(None, ("dp", "ctx")),
        P(None, ("dp", "ctx"), None),
        P(None, ("dp", "ctx")),
        P(None, ("dp", "ctx")),
        P(None, ("dp", "ctx")),
        P(None, ("dp", "ctx"), None),
        P(None, ("dp", "ctx")),
        P(None, ("dp", "ctx"), None),
        P(None, ("dp", "ctx")),
    )
    return jax.shard_map(
        on_device, mesh=mesh, in_specs=in_specs, out_specs=out_specs, check_vma=False
    )
```

time: 1690 us -> 832 us (0.49)
  blocking collectives: 422 us -> 16.7 us
  waiting for transfers between devices: 854 us -> 462 us
  matrix products: 194 us -> 128 us
  other arithmetic: 79.4 us -> 38 us
  starting transfers between devices: 0.85 us -> 32.1 us
  local copies, waits for them, and re-layouts: 99.7 us -> 128 us
  loops' own time: 17.5 us -> 0 us
    reduce_scatter x6 -> x2, waiting for transfers between devices: 764 us -> 224 us  [scatter_layer(): lax.psum_scatter(pad_rows(packed), ('dp', 'ctx'), scatter_dimension=0, ti...]
    all_gather x14 -> x1, blocking collectives: 381 us -> 16.7 us  [on_device(): lax.all_gather(segments[0].astype(jnp.bfloat16), 'ctx', axis=0, tiled=True)]
    all_gather x14 -> x2, waiting for transfers between devices: 85.1 us -> 207 us  [gather_layer(): whole = lax.all_gather(pad_rows(packed), ('dp', 'ctx'), axis=0, tiled=False)]
    dot_general x20 -> x12, matrix products: 104 us -> 61.5 us  [head_dot(): lax.dot_general(left_op, right_op, (((left_dim,), (right_dim,)), ((0,), (...]
    unnamed x1 -> x0, blocking collectives: 40.6 us -> none
    slice x10 -> x38, local copies, waits for them, and re-layouts: 5.81 us -> 45.4 us  [the longest x4 23.2 us: taken(): return whole[:, first:first + count].reshape(-1, width)]
    all_to_all x0 -> x8, starting transfers between devices: none -> 31.8 us  [the longest x4 16 us: from_heads(): got = lax.all_to_all(sent, 'ctx', 0, 0, tiled=True)]
    all_to_all x0 -> x8, waiting for transfers between devices: none -> 31 us  [the longest x4 20 us: to_heads(): got = lax.all_to_all(sent, 'ctx', 0, 0, tiled=True)]
  transfers between devices with their start and end apart: 21 -> 12, of which waited for: 9 -> 11; matrix products, arithmetic and copies ran while one was open for 21% -> 16% of each run, Pallas kernels for 0% -> 0%
where the time goes in v1:
time: 832 us; the launch traced here: 821 us
  waiting for transfers between devices  462 us (56%)
  local copies, waits for them, and re-layouts  128 us (15%)
  matrix products  128 us (15%)
  other arithmetic  38 us (5%)
  starting transfers between devices  32.1 us (4%)
  blocking collectives  16.7 us (2%)
  between operations  16.1 us (2%)
    reduce_scatter x2, waiting for transfers between devices, scatter_layer(): lax.psum_scatter(pad_rows(packed), ('dp', 'ctx'), scatter_dimension=0, ti...  224 us
    all_gather x2, waiting for transfers between devices, gather_layer(): whole = lax.all_gather(pad_rows(packed), ('dp', 'ctx'), axis=0, tiled=False)  207 us
    dot_general x12, matrix products, head_dot(): lax.dot_general(left_op, right_op, (((left_dim,), (right_dim,)), ((0,), (...  61.5 us
    dot_general x8, matrix products, contract_rows(): lax.dot_general(left_op, right_op, (((0,), (0,)), ((), ())), preferred_el...  26.6 us
    unnamed x254, local copies, waits for them, and re-layouts  25.9 us
    slice x4, local copies, waits for them, and re-layouts, taken(): return whole[:, first:first + count].reshape(-1, width)  23.2 us
    dot_general x8, matrix products, matmul(): return jnp.dot(left_op, right_op, preferred_element_type=jnp.float32)  21.2 us
    all_to_all x4, waiting for transfers between devices, to_heads(): got = lax.all_to_all(sent, 'ctx', 0, 0, tiled=True)  20 us
  transfers between devices with their start and end apart: 12, of which 11 were waited for; matrix products, arithmetic and copies ran while one was open for 16% of the time, Pallas kernels for 0%

profile of v1, /device:TPU:0, one launch (start us, length us, event | category | flops | bytes accessed | tf_op | source)
XLA Modules:
  0.0 821.2 jit_solution(16681104765465733664)
XLA Ops:
  18.6 108.0 %all-gather.6.cloned.1.call-done = bf16[9728,768]{1,0:T(8,128)(2,1)} async-done(((bf16[304,768]{1,0:T(8,128)(2,1)}), bf16[9728,768]{1,0:T(8,128)(2,1)}) %all-gather.6.cloned.1.call-update) | async-done | bytes 14942224 | tf_op jit(solution)/shard_map/all_gather | solution.py:224
  129.4 6.6 fusion.115
  136.0 98.8 %all-gather.8.cloned.1.call-done = bf16[9728,768]{1,0:T(8,128)(2,1)} async-done(((bf16[304,768]{1,0:T(8,128)(2,1)}), bf16[9728,768]{1,0:T(8,128)(2,1)}) %all-gather.8.cloned.1.call-update) | async-done | bytes 14942224 | tf_op jit(solution)/shard_map/all_gather | solution.py:224
  246.6 16.7 %all-gather = bf16[1,1024]{1,0:T(2,128)(2,1)S(1)} all-gather(bf16[1,256]{1,0:T(2,128)(2,1)S(1)} %convert_element_type.401), channel_id=2, replica_groups=mesh['dp'=8,'ctx'=4] {'ctx'}, dimensions={1}, use_global_device_ids=true | all-gather | bytes 2560 | tf_op jit(solution)/shard_map/all_gather | solution.py:311
  284.4 5.5 fusion.130
  295.6 7.0 fusion.114
  318.4 15.6 %all-to-all-done.2 = bf16[4,3,256,192]{2,3,1,0:T(8,128)(2,1)S(1)} async-done(((bf16[4,3,256,192]{2,3,1,0:T(8,128)(2,1)}), bf16[4,3,256,192]{2,3,1,0:T(8,128)(2,1)S(1)}, u32[]{:S(2)}, u32[]{:S(2)}) %all-to-all-start.2) | async-done | bytes 1179680 | tf_op jit(solution)/shard_map/all_to_all | solution.py:53
  346.1 5.4 fusion.133
  358.1 4.9 slice.768
  365.6 5.4 convolution_add_fusion.2
  382.8 5.3 convolution_convert_fusion.1
  393.8 7.3 fusion.43
  401.1 7.3 multiply_convert_fusion.1
  458.1 6.2 pad.35
  466.8 5.9 fusion.136
  483.6 5.2 convolution_convert_fusion.4
  494.2 7.9 multiply_convert_fusion
  508.8 4.9 fusion.51
  514.7 8.6 %fusion.46 = bf16[3,1024,64]{1,2,0:T(8,128)(2,1)S(1)} fusion(bf16[3,1024,64]{1,2,0:T(8,128)(2,1)} %copy-done.39, f32[3,1024,1024]{1,2,0:T(8,128)} %copy-done, f32[3,1024]{1,0:T(4,128)S(1)} %log_add_fusion, pred[1024,1024]{0,1:T(8,128)(4,1)S(1)} %copy-done.2), kind=kOutput, calls=%fused_computation.80 | convolution fusion | flops 415432704 | bytes 14430208 | tf_op jit(solution)/shard_map/dot_general | solution.py:70
  533.4 4.8 fusion.116
  559.2 6.3 pad.33
  566.3 6.0 fusion.54
  573.6 55.7 %reduce-scatter.5.cloned.1.call-done = bf16[1,304,768]{2,1,0:T(8,128)(2,1)} async-done(((bf16[32,304,768]{2,1,0:T(8,128)(2,1)}), bf16[1,304,768]{2,1,0:T(8,128)(2,1)}) %reduce-scatter.5.cloned.1.call-update) | async-done | bytes 466960 | tf_op jit(solution)/shard_map/reduce_scatter | solution.py:257
  633.1 168.7 %reduce-scatter.3.cloned.1.call-done = bf16[1,304,768]{2,1,0:T(8,128)(2,1)} async-done(((bf16[32,304,768]{2,1,0:T(8,128)(2,1)}), bf16[1,304,768]{2,1,0:T(8,128)(2,1)}) %reduce-scatter.3.cloned.1.call-update) | async-done | bytes 466960 | tf_op jit(solution)/shard_map/reduce_scatter | solution.py:257
  (495 shorter events, 231.1 us)
Async XLA Ops:
  7.2 11.0 %copy-start.13 = (bf16[1,256,768]{2,1,0:T(8,128)(2,1)S(1)}, bf16[1,256,768]{2,1,0:T(8,128)(2,1)}, u32[]{:S(2)}) copy-start(bf16[1,256,768]{2,1,0:T(8,128)(2,1)} %param.18) | copy-start | bytes 1179652
  7.2 119.4 %all-gather.6.cloned.1.call-start = ((), (), s32[]{:S(2)}) async-start(), calls=%async_computation.12 | async-start | bytes 15409152 | tf_op jit(solution)/shard_map/all_gather | solution.py:224
  17.2 217.6 %all-gather.8.cloned.1.call-start = ((), (), s32[]{:S(2)}) async-start(), calls=%async_computation.13 | async-start | bytes 15409152 | tf_op jit(solution)/shard_map/all_gather | solution.py:224
  18.3 220.3 %copy-start.82 = (f32[256]{0:T(256)}, f32[256]{0:T(256)S(1)}, u32[]{:S(2)}) copy-start(f32[256]{0:T(256)S(1)} %broadcast_multiply_fusion.11) | copy-start | bytes 3076
  18.6 220.1 %copy-start.86 = (f32[256]{0:T(256)}, f32[256]{0:T(256)S(1)}, u32[]{:S(2)}) copy-start(f32[256]{0:T(256)S(1)} %add_rsqrt_fusion.3) | copy-start | bytes 3076
  129.3 109.4 %copy-start.74 = (f32[768]{0:T(1024)}, f32[768]{0:T(1024)S(1)}, u32[]{:S(2)}) copy-start(f32[768]{0:T(1024)S(1)} %reshape.728) | copy-start | bytes 9220
  129.4 109.3 %copy-start.91 = (f32[768]{0:T(1024)}, f32[768]{0:T(1024)S(1)}, u32[]{:S(2)}) copy-start(f32[768]{0:T(1024)S(1)} %reshape.729) | copy-start | bytes 9220
  136.0 102.7 %copy-start.42 = (bf16[32,24,768]{2,1,0:T(8,128)(2,1)}, bf16[32,24,768]{2,1,0:T(8,128)(2,1)S(1)}, u32[]{:S(2)}) copy-start(bf16[32,24,768]{2,1,0:T(8,128)(2,1)S(1)} %get-tuple-element.52) | copy-start | bytes 3538948
  136.0 102.7 %copy-start.44 = (bf16[32,24,768]{2,1,0:T(8,128)(2,1)}, bf16[32,24,768]{2,1,0:T(8,128)(2,1)S(1)}, u32[]{:S(2)}) copy-start(bf16[32,24,768]{2,1,0:T(8,128)(2,1)S(1)} %get-tuple-element.53) | copy-start | bytes 3538948
  243.0 28.6 %all-to-all-start = ((bf16[4,3,256,192]{2,3,1,0:T(8,128)(2,1)}), bf16[4,3,256,192]{2,3,1,0:T(8,128)(2,1)S(1)}, u32[]{:S(2)}, u32[]{:S(2)}) async-start(bf16[4,3,256,192]{2,3,1,0:T(8,128)(2,1)} %copy.86), calls=%async_computation | async-start | bytes 2359296 | tf_op jit(solution)/shard_map/all_to_all | solution.py:53
  271.5 39.0 %copy-start.76 = (f32[768]{0:T(1024)}, f32[768]{0:T(1024)S(1)}, u32[]{:S(2)}) copy-start(f32[768]{0:T(1024)S(1)} %reshape.735) | copy-start | bytes 9220
  271.6 38.9 %copy-start.93 = (f32[768]{0:T(1024)}, f32[768]{0:T(1024)S(1)}, u32[]{:S(2)}) copy-start(f32[768]{0:T(1024)S(1)} %reshape.736) | copy-start | bytes 9220
  292.0 11.0 %all-to-all-start.1 = ((bf16[4,1,256,192]{2,3,1,0:T(8,128)(2,1)}), bf16[4,1,256,192]{2,3,1,0:T(8,128)(2,1)S(1)}, u32[]{:S(2)}, u32[]{:S(2)}) async-start(bf16[4,1,256,192]{2,3,1,0:T(8,128)(2,1)} %bitcast.29), calls=%async_computation.1 | async-start | bytes 786432 | tf_op jit(solution)/shard_map/all_to_all | solution.py:64
  314.5 19.6 %all-to-all-start.2 = ((bf16[4,3,256,192]{2,3,1,0:T(8,128)(2,1)}), bf16[4,3,256,192]{2,3,1,0:T(8,128)(2,1)S(1)}, u32[]{:S(2)}, u32[]{:S(2)}) async-start(bf16[4,3,256,192]{2,3,1,0:T(8,128)(2,1)} %copy.96), calls=%async_computation.2 | async-start | bytes 2359296 | tf_op jit(solution)/shard_map/all_to_all | solution.py:53
  353.6 11.1 %all-to-all-start.3 = ((bf16[4,1,256,192]{2,3,1,0:T(8,128)(2,1)}), bf16[4,1,256,192]{2,3,1,0:T(8,128)(2,1)S(1)}, u32[]{:S(2)}, u32[]{:S(2)}) async-start(bf16[4,1,256,192]{2,3,1,0:T(8,128)(2,1)} %bitcast.66), calls=%async_computation.3 | async-start | bytes 786432 | tf_op jit(solution)/shard_map/all_to_all | solution.py:64
  378.9 11.3 %all-to-all-start.4 = ((bf16[4,1,256,192]{2,3,1,0:T(8,128)(2,1)}), bf16[4,1,256,192]{2,3,1,0:T(8,128)(2,1)S(1)}, u32[]{:S(2)}, u32[]{:S(2)}) async-start(bf16[4,1,256,192]{2,3,1,0:T(8,128)(2,1)} %bitcast.81), calls=%async_computation.4 | async-start | bytes 786432 | tf_op jit(solution)/shard_map/all_to_all | solution.py:53
  382.8 11.0 %copy-start.2 = (pred[1024,1024]{0,1:T(8,128)(4,1)S(1)}, pred[1024,1024]{0,1:T(8,128)(4,1)}, u32[]{:S(2)}) copy-start(pred[1024,1024]{0,1:T(8,128)(4,1)} %fusion.20) | copy-start | bytes 3145732
  421.9 20.2 %all-to-all-start.5 = ((bf16[4,3,256,192]{2,3,1,0:T(8,128)(2,1)}), bf16[4,3,256,192]{2,3,1,0:T(8,128)(2,1)}, u32[]{:S(2)}, u32[]{:S(2)}) async-start(bf16[4,3,256,192]{2,3,1,0:T(8,128)(2,1)} %bitcast.394), calls=%async_computation.5 | async-start | bytes 2359296 | tf_op jit(solution)/shard_map/all_to_all | solution.py:64
  426.2 203.1 %reduce-scatter.5.cloned.1.call-start = ((), (), s32[]{:S(2)}) async-start(), calls=%async_computation.11 | async-start | bytes 15409152 | tf_op jit(solution)/shard_map/reduce_scatter | solution.py:257
  479.1 12.0 %all-to-all-start.6 = ((bf16[4,1,256,192]{2,3,1,0:T(8,128)(2,1)}), bf16[4,1,256,192]{2,3,1,0:T(8,128)(2,1)}, u32[]{:S(2)}, u32[]{:S(2)}) async-start(bf16[4,1,256,192]{2,3,1,0:T(8,128)(2,1)} %bitcast.423), calls=%async_computation.6 | async-start | bytes 786432 | tf_op jit(solution)/shard_map/all_to_all | solution.py:53
  494.2 10.5 %copy-start.27 = (bf16[3,1024,64]{1,2,0:T(8,128)(2,1)S(1)}, bf16[3,1024,64]{1,2,0:T(8,128)(2,1)}, u32[]{:S(2)}) copy-start(bf16[3,1024,64]{1,2,0:T(8,128)(2,1)} %squeeze.153) | copy-start | bytes 1179652
  526.9 20.4 %all-to-all-start.7 = ((bf16[4,3,256,192]{2,3,1,0:T(8,128)(2,1)}), bf16[4,3,256,192]{2,3,1,0:T(8,128)(2,1)}, u32[]{:S(2)}, u32[]{:S(2)}) async-start(bf16[4,3,256,192]{2,3,1,0:T(8,128)(2,1)} %bitcast.393), calls=%async_computation.7 | async-start | bytes 2359296 | tf_op jit(solution)/shard_map/all_to_all | solution.py:64
  531.3 270.5 %reduce-scatter.3.cloned.1.call-start = ((), (), s32[]{:S(2)}) async-start(), calls=%async_computation.10 | async-start | bytes 15409152 | tf_op jit(solution)/shard_map/reduce_scatter | solution.py:257
  801.8 9.0 %copy-start.34 = (bf16[1,304,768]{2,1,0:T(8,128)(2,1)S(1)}, bf16[1,304,768]{2,1,0:T(8,128)(2,1)}, u32[]{:S(2)}) copy-start(bf16[1,304,768]{2,1,0:T(8,128)(2,1)} %reduce-scatter.3.cloned.1.call-done) | copy-start | bytes 1400836
  (99 other events, 377.7 us)
Sparse Core Ops, SparseCore 0:
  17.3 109.2 all-gather.5
  130.1 104.7 all-gather.7
  464.5 164.7 reduce-scatter.4
  636.3 165.4 reduce-scatter.2

commit v2 on v1

--- a/solution.py
+++ b/solution.py
@@ -203,25 +203,28 @@
     return [matrix[..., c : c + width] for c in range(0, matrix.shape[-1], width)]
 
 
-def pad_rows(packed):
-    rows = packed.shape[-2]
-    return jnp.pad(packed, ((0, 0),) * (packed.ndim - 2) + ((0, -rows % 16), (0, 0)))
-
-
-def pack_vectors(vectors, width):
+def pack_vectors(vectors, width, rows_before):
     joined = jnp.concatenate(vectors, axis=-1)
     short = -joined.shape[-1] % width
+    rows = (joined.shape[-1] + short) // width
+    short += width * (-(rows_before + rows) % 16)
     joined = jnp.pad(joined, ((0, 0),) * (joined.ndim - 1) + ((0, short),))
     return joined.reshape(joined.shape[:-1] + (-1, width))
 
 
 def gather_layer(matrices, vectors):
+    w_query, w_key, w_value, w_out, w_up, w_down = matrices
+    width = w_query.shape[1]
+    pieces = [w_query, w_key, w_value, w_out] + column_pieces(w_up, width) + [w_down]
+    pieces.append(pack_vectors(vectors, width, sum(p.shape[0] for p in pieces)))
+    packed = jnp.concatenate(pieces, axis=0)
+    return lax.all_gather(packed, ("dp", "ctx"), axis=0, tiled=False)
+
+
+def unpack_layer(whole, matrices, vectors):
     w_query, w_key, w_value, w_out, w_up, w_down = matrices
     rows, width = w_query.shape
     up_count = w_up.shape[1] // width
-    pieces = [w_query, w_key, w_value, w_out] + column_pieces(w_up, width)
-    packed = jnp.concatenate(pieces + [w_down, pack_vectors(vectors, width)], axis=0)
-    whole = lax.all_gather(pad_rows(packed), ("dp", "ctx"), axis=0, tiled=False)
 
     def taken(first, count):
         return whole[:, first : first + count].reshape(-1, width)
@@ -245,46 +248,60 @@
     )
 
 
-def scatter_layer(terms):
-    g_proj, g_w_out, g_w_up, g_w_down, g_vectors = terms
-    width = g_w_out.shape[1]
+def scatter_terms(blocks, vectors):
+    width = blocks[0].shape[1]
     shards = lax.axis_size(("dp", "ctx"))
-    blocks = column_pieces(g_proj, width) + [g_w_out] + column_pieces(g_w_up, width) + [g_w_down]
     blocks = [b.astype(jnp.bfloat16).reshape(shards, -1, width) for b in blocks]
-    rows, down_rows = blocks[0].shape[1], blocks[-1].shape[1]
-    vectors = [v.astype(jnp.bfloat16).reshape(shards, -1) for v in g_vectors]
-    packed = jnp.concatenate(blocks + [pack_vectors(vectors, width)], axis=1)
+    vectors = [v.astype(jnp.bfloat16).reshape(shards, -1) for v in vectors]
+    last = pack_vectors(vectors, width, sum(b.shape[1] for b in blocks))
     own = lax.psum_scatter(
-        pad_rows(packed), ("dp", "ctx"), scatter_dimension=0, tiled=False
+        jnp.concatenate(blocks + [last], axis=1),
+        ("dp", "ctx"),
+        scatter_dimension=0,
+        tiled=False,
     ).astype(jnp.float32)
-    up_count = len(blocks) - 5
-    parts = [own[i * rows : (i + 1) * rows] for i in range(4 + up_count)]
-    start = (4 + up_count) * rows
-    down = own[start : start + down_rows]
-    flat = own[start + down_rows :].reshape(-1)
-    out_vectors = []
+    out_blocks, out_vectors = [], []
+    start = 0
+    for block in blocks:
+        out_blocks.append(own[start : start + block.shape[1]])
+        start += block.shape[1]
+    flat = own[start:].reshape(-1)
     place = 0
     for vector in vectors:
         out_vectors.append(flat[place : place + vector.shape[1]])
         place += vector.shape[1]
-    gain_one, shift_one, b_query, b_value, b_out, gain_two, shift_two, b_down, b_up = out_vectors
-    return (
-        gain_one,
-        shift_one,
-        parts[0],
-        b_query,
-        parts[1],
-        parts[2],
-        b_value,
-        parts[3],
-        b_out,
-        gain_two,
-        shift_two,
-        jnp.concatenate(parts[4:], axis=1),
-        b_up,
-        down,
-        b_down,
-    )
+    return out_blocks, out_vectors
+
+
+def scatter_all(collected):
+    early, late = [], []
+    for layer_no in reversed(range(len(collected))):
+        g_proj, g_w_out, g_w_up, g_w_down, g_vectors = collected[layer_no]
+        width = g_w_out.shape[1]
+        feed = (layer_no, 0, [g_w_out] + column_pieces(g_w_up, width) + [g_w_down], g_vectors[4:])
+        attn = (layer_no, 1, column_pieces(g_proj, width), g_vectors[:4])
+        (late if early else early).append(feed)
+        late.append(attn)
+    found = {}
+    for group in (early, late):
+        blocks, vectors = scatter_terms(
+            [b for entry in group for b in entry[2]], [v for entry in group for v in entry[3]]
+        )
+        for layer_no, kind, in_blocks, in_vectors in group:
+            found[layer_no, kind] = (blocks[: len(in_blocks)], vectors[: len(in_vectors)])
+            blocks, vectors = blocks[len(in_blocks) :], vectors[len(in_vectors) :]
+    results = []
+    for layer_no in range(len(collected)):
+        feed, feed_vectors = found[layer_no, 0]
+        proj, proj_vectors = found[layer_no, 1]
+        gain_one, shift_one, b_query, b_value = proj_vectors
+        b_out, gain_two, shift_two, b_down, b_up = feed_vectors
+        up = jnp.concatenate(feed[1:-1], axis=1)
+        results.append(
+            (gain_one, shift_one, proj[0], b_query, proj[1], proj[2], b_value)
+            + (feed[0], b_out, gain_two, shift_two, up, b_up, feed[-1], b_down)
+        )
+    return results
 
 
 def on_device(
@@ -314,13 +331,16 @@
     allowed = (place[None, :] <= place[:, None]) & (seg_all[None, :] == seg_all[:, None])
     matrices = (w_query, w_key, w_value, w_out, w_up, w_down)
     vectors = (ln1_gain, ln1_bias, b_query, b_value, b_out, ln2_gain, ln2_bias, b_down, b_up)
-    every_layer = [
-        gather_layer([m[l] for m in matrices], [v[l] for v in vectors])
-        for l in range(layer_count)
-    ]
+    shards = [([m[l] for m in matrices], [v[l] for v in vectors]) for l in range(layer_count)]
+    packed = [gather_layer(*own) for own in shards]
+    every_layer = []
     stream = tokens[0].astype(jnp.float32)
     kept_acts = []
     for layer_no in range(layer_count):
+        whole = packed[layer_no]
+        if layer_no > 0:
+            stream, whole = lax.optimization_barrier((stream, whole))
+        every_layer.append(unpack_layer(whole, *shards[layer_no]))
         stream, saved_acts = layer_forward(stream, allowed, every_layer[layer_no])
         kept_acts.append(saved_acts)
     output = stream.astype(jnp.bfloat16)[None]
@@ -330,8 +350,8 @@
         grad_stream, terms = layer_back(
             grad_stream, allowed, every_layer[layer_no], kept_acts[layer_no]
         )
-        collected[layer_no] = scatter_layer(terms)
-    stacked = tuple(jnp.stack(members) for members in zip(*collected))
+        collected[layer_no] = terms
+    stacked = tuple(jnp.stack(members) for members in zip(*scatter_all(collected)))
     return (output, grad_stream[None]) + stacked
 
 

time: 832 us -> 739 us (0.89)
  waiting for transfers between devices: 462 us -> 371 us
    all_gather x2, waiting for transfers between devices: 207 us -> 139 us  [gather_layer(): return lax.all_gather(packed, ('dp', 'ctx'), axis=0, tiled=False)]
    reduce_scatter x2, waiting for transfers between devices: 224 us -> 187 us  [scatter_terms(): lax.psum_scatter(jnp.concatenate(blocks + [last], axis=1), ('dp', 'ctx'),...]
    unnamed x254 -> x242, local copies, waits for them, and re-layouts: 25.9 us -> 46.7 us
    all_to_all x4, waiting for transfers between devices: 11 us -> 29.3 us  [from_heads(): got = lax.all_to_all(sent, 'ctx', 0, 0, tiled=True)]
    pad x4 -> x0, local copies, waits for them, and re-layouts: 14.1 us -> none  [pad_rows(): jnp.pad(packed, ((0, 0),) * (packed.ndim - 2) + ((0, -rows % 16), (0, 0)))]
  transfers between devices with their start and end apart: 12 -> 12, of which waited for: 11 -> 8; matrix products, arithmetic and copies ran while one was open for 16% -> 27% of each run, Pallas kernels for 0% -> 0%
where the time goes in v2:
time: 739 us; the launch traced here: 728 us
  waiting for transfers between devices  371 us (50%)
  local copies, waits for them, and re-layouts  131 us (18%)
  matrix products  124 us (17%)
  other arithmetic  36.2 us (5%)
  starting transfers between devices  32.4 us (4%)
  blocking collectives  17.7 us (2%)
  between operations  15.9 us (2%)
    reduce_scatter x2, waiting for transfers between devices, scatter_terms(): lax.psum_scatter(jnp.concatenate(blocks + [last], axis=1), ('dp', 'ctx'),...  187 us
    all_gather x2, waiting for transfers between devices, gather_layer(): return lax.all_gather(packed, ('dp', 'ctx'), axis=0, tiled=False)  139 us
    dot_general x12, matrix products, head_dot(): lax.dot_general(left_op, right_op, (((left_dim,), (right_dim,)), ((0,), (...  65.2 us
    unnamed x242, local copies, waits for them, and re-layouts  46.7 us
    all_to_all x4, waiting for transfers between devices, from_heads(): got = lax.all_to_all(sent, 'ctx', 0, 0, tiled=True)  29.3 us
    slice x4, local copies, waits for them, and re-layouts, taken(): return whole[:, first:first + count].reshape(-1, width)  23.5 us
    dot_general x8, matrix products, matmul(): return jnp.dot(left_op, right_op, preferred_element_type=jnp.float32)  23 us
    dot_general x8, matrix products, contract_rows(): lax.dot_general(left_op, right_op, (((0,), (0,)), ((), ())), preferred_el...  19.9 us
  transfers between devices with their start and end apart: 12, of which 8 were waited for; matrix products, arithmetic and copies ran while one was open for 27% of the time, Pallas kernels for 0%

profile of v2, /device:TPU:0, one launch (start us, length us, event | category | flops | bytes accessed | tf_op | source)
XLA Modules:
  0.0 728.3 jit_solution(18404083198914333791)
XLA Ops:
  18.7 107.9 %all-gather.6.cloned.1.call-done = bf16[9728,768]{1,0:T(8,128)(2,1)} async-done(((bf16[304,768]{1,0:T(8,128)(2,1)}), bf16[9728,768]{1,0:T(8,128)(2,1)}) %all-gather.6.cloned.1.call-update) | async-done | bytes 14942224 | tf_op jit(solution)/shard_map/all_gather | solution.py:221
  130.1 6.4 fusion.115
  143.7 17.7 %all-gather = bf16[1,1024]{1,0:T(2,128)(2,1)S(1)} all-gather(bf16[1,256]{1,0:T(2,128)(2,1)S(1)} %convert_element_type.396), channel_id=2, replica_groups=mesh['dp'=8,'ctx'=4] {'ctx'}, dimensions={1}, use_global_device_ids=true | all-gather | bytes 2560 | tf_op jit(solution)/shard_map/all_gather | solution.py:328
  171.2 4.4 fusion
  175.8 5.5 fusion.129
  187.2 5.5 slice.739
  194.0 5.0 all-to-all-done.1
  207.9 31.1 %all-gather.8.cloned.1.call-done = bf16[9728,768]{1,0:T(8,128)(2,1)} async-done(((bf16[304,768]{1,0:T(8,128)(2,1)}), bf16[9728,768]{1,0:T(8,128)(2,1)}) %all-gather.8.cloned.1.call-update) | async-done | bytes 14942224 | tf_op jit(solution)/shard_map/all_gather | solution.py:221
  240.1 6.7 fusion.114
  257.9 15.6 %all-to-all-done.2 = bf16[4,3,256,192]{2,3,1,0:T(8,128)(2,1)S(1)} async-done(((bf16[4,3,256,192]{2,3,1,0:T(8,128)(2,1)}), bf16[4,3,256,192]{2,3,1,0:T(8,128)(2,1)S(1)}, u32[]{:S(2)}, u32[]{:S(2)}) %all-to-all-start.2) | async-done | bytes 1179680 | tf_op jit(solution)/shard_map/all_to_all | solution.py:53
  280.9 4.5 fusion.2
  285.6 5.4 fusion.131
  297.8 4.9 slice.640
  306.5 5.4 convolution_add_fusion.2
  321.1 4.4 convolution_convert_fusion
  352.9 9.6 %fusion.43 = bf16[3,1024,64]{1,2,0:T(8,128)(2,1)} fusion(bf16[3,1024,64]{1,2,0:T(8,128)(2,1)} %squeeze_reshape.14, f32[3,1024,1024]{1,2,0:T(8,128)} %copy-done.1, f32[3,1024]{1,0:T(4,128)S(1)} %log_add_fusion.1, pred[1024,1024]{0,1:T(8,128)(4,1)S(1)} %copy-done.2), kind=kOutput, calls=%fused_computation.79 | convolution fusion | flops 415432704 | bytes 14430208 | tf_op jit(solution)/shard_map/dot_general | solution.py:70
  362.5 7.7 %multiply_convert_fusion.1 = bf16[3,1024,1024]{1,2,0:T(8,128)(2,1)S(1)} fusion(f32[3,1024,1024]{1,2,0:T(8,128)} %copy-done.1, f32[3,1024]{1,0:T(4,128)S(1)} %multiply_reduce_fusion.6, f32[3,1024]{1,0:T(4,128)S(1)} %log_add_fusion.1, pred[1024,1024]{0,1:T(8,128)(4,1)S(1)} %copy-done.2, bf16[3,1024,64]{1,2,0:T(8,128)(2,1)S(1)} %copy-done.36, ...), kind=kOutput, calls=%fused_computation.2 | convolution fusion | flops 421527552 | bytes 20733952 | tf_op jit(solution)/shard_map/dot_general | solution.py:70
  384.6 4.6 all-to-all-start.5
  389.3 19.6 %all-to-all-done.5 = bf16[4,3,256,192]{2,3,1,0:T(8,128)(2,1)} async-done(((bf16[4,3,256,192]{2,3,1,0:T(8,128)(2,1)}), bf16[4,3,256,192]{2,3,1,0:T(8,128)(2,1)}, u32[]{:S(2)}, u32[]{:S(2)}) %all-to-all-start.5) | async-done | bytes 1179680 | tf_op jit(solution)/shard_map/all_to_all | solution.py:64
  445.5 7.7 %multiply_convert_fusion = bf16[3,1024,1024]{1,2,0:T(8,128)(2,1)S(1)} fusion(f32[3,1024,1024]{1,2,0:T(8,128)} %copy-done, f32[3,1024]{1,0:T(4,128)S(1)} %multiply_reduce_fusion.3, f32[3,1024]{1,0:T(4,128)S(1)} %log_add_fusion, pred[1024,1024]{0,1:T(8,128)(4,1)S(1)} %copy-done.2, bf16[3,1024,64]{1,2,0:T(8,128)(2,1)S(1)} %squeeze_reshape.15, ...), kind=kOutput, calls=%fused_computation | convolution fusion | flops 421527552 | bytes 20733952 | tf_op jit(solution)/shard_map/dot_general | solution.py:70
  459.1 5.6 fusion.51
  466.0 9.0 %fusion.46 = bf16[3,1024,64]{1,2,0:T(8,128)(2,1)} fusion(bf16[3,1024,64]{1,2,0:T(8,128)(2,1)} %copy-done.35, f32[3,1024,1024]{1,2,0:T(8,128)} %copy-done, f32[3,1024]{1,0:T(4,128)S(1)} %log_add_fusion, pred[1024,1024]{0,1:T(8,128)(4,1)S(1)} %copy-done.2), kind=kOutput, calls=%fused_computation.80 | convolution fusion | flops 415432704 | bytes 14430208 | tf_op jit(solution)/shard_map/dot_general | solution.py:70
  511.1 6.1 fusion.54
  522.1 186.7 %reduce-scatter.3.cloned.1.call-done = bf16[1,368,768]{2,1,0:T(8,128)(2,1)} async-done(((bf16[32,368,768]{2,1,0:T(8,128)(2,1)}), bf16[1,368,768]{2,1,0:T(8,128)(2,1)}) %reduce-scatter.3.cloned.1.call-update) | async-done | bytes 565264 | tf_op jit(solution)/shard_map/reduce_scatter | solution.py:257
  (483 shorter events, 224.9 us)
Async XLA Ops:
  7.2 11.0 %copy-start.13 = (bf16[1,256,768]{2,1,0:T(8,128)(2,1)S(1)}, bf16[1,256,768]{2,1,0:T(8,128)(2,1)}, u32[]{:S(2)}) copy-start(bf16[1,256,768]{2,1,0:T(8,128)(2,1)} %param.18) | copy-start | bytes 1179652
  7.2 119.4 %all-gather.6.cloned.1.call-start = ((), (), s32[]{:S(2)}) async-start(), calls=%async_computation.12 | async-start | bytes 15409152 | tf_op jit(solution)/shard_map/all_gather | solution.py:221
  17.2 221.8 %all-gather.8.cloned.1.call-start = ((), (), s32[]{:S(2)}) async-start(), calls=%async_computation.13 | async-start | bytes 15409152 | tf_op jit(solution)/shard_map/all_gather | solution.py:221
  18.4 118.1 %copy-start.80 = (f32[256]{0:T(256)}, f32[256]{0:T(256)S(1)}, u32[]{:S(2)}) copy-start(f32[256]{0:T(256)S(1)} %broadcast_multiply_fusion.11) | copy-start | bytes 3076
  18.6 117.9 %copy-start.84 = (f32[256]{0:T(256)}, f32[256]{0:T(256)S(1)}, u32[]{:S(2)}) copy-start(f32[256]{0:T(256)S(1)} %add_rsqrt_fusion.3) | copy-start | bytes 3076
  140.2 22.9 %all-to-all-start = ((bf16[4,3,256,192]{2,3,1,0:T(8,128)(2,1)}), bf16[4,3,256,192]{2,3,1,0:T(8,128)(2,1)S(1)}, u32[]{:S(2)}, u32[]{:S(2)}) async-start(bf16[4,3,256,192]{2,3,1,0:T(8,128)(2,1)} %copy.84), calls=%async_computation | async-start | bytes 2359296 | tf_op jit(solution)/shard_map/all_to_all | solution.py:53
  183.5 15.6 %all-to-all-start.1 = ((bf16[4,1,256,192]{2,3,1,0:T(8,128)(2,1)}), bf16[4,1,256,192]{2,3,1,0:T(8,128)(2,1)S(1)}, u32[]{:S(2)}, u32[]{:S(2)}) async-start(bf16[4,1,256,192]{2,3,1,0:T(8,128)(2,1)} %bitcast.29), calls=%async_computation.1 | async-start | bytes 786432 | tf_op jit(solution)/shard_map/all_to_all | solution.py:64
  187.2 11.9 %copy-start.10 = (bf16[32,24,768]{2,1,0:T(8,128)(2,1)S(1)}, bf16[32,24,768]{2,1,0:T(8,128)(2,1)}, u32[]{:S(2)}) copy-start(bf16[32,24,768]{2,1,0:T(8,128)(2,1)} %get-tuple-element.55) | copy-start | bytes 3538948
  207.9 41.6 %copy-start.6 = (f32[256,768]{1,0:T(8,128)}, f32[256,768]{1,0:T(8,128)S(1)}, u32[]{:S(2)}) copy-start(f32[256,768]{1,0:T(8,128)S(1)} %fusion.42) | copy-start | bytes 2359300
  254.2 19.4 %all-to-all-start.2 = ((bf16[4,3,256,192]{2,3,1,0:T(8,128)(2,1)}), bf16[4,3,256,192]{2,3,1,0:T(8,128)(2,1)S(1)}, u32[]{:S(2)}, u32[]{:S(2)}) async-start(bf16[4,3,256,192]{2,3,1,0:T(8,128)(2,1)} %copy.94), calls=%async_computation.2 | async-start | bytes 2359296 | tf_op jit(solution)/shard_map/all_to_all | solution.py:53
  293.1 11.3 %all-to-all-start.3 = ((bf16[4,1,256,192]{2,3,1,0:T(8,128)(2,1)}), bf16[4,1,256,192]{2,3,1,0:T(8,128)(2,1)S(1)}, u32[]{:S(2)}, u32[]{:S(2)}) async-start(bf16[4,1,256,192]{2,3,1,0:T(8,128)(2,1)} %bitcast.66), calls=%async_computation.3 | async-start | bytes 786432 | tf_op jit(solution)/shard_map/all_to_all | solution.py:64
  330.7 16.5 %all-to-all-start.4 = ((bf16[4,1,256,192]{2,3,1,0:T(8,128)(2,1)}), bf16[4,1,256,192]{2,3,1,0:T(8,128)(2,1)}, u32[]{:S(2)}, u32[]{:S(2)}) async-start(bf16[4,1,256,192]{2,3,1,0:T(8,128)(2,1)} %bitcast.81), calls=%async_computation.4 | async-start | bytes 786432 | tf_op jit(solution)/shard_map/all_to_all | solution.py:53
  334.8 183.6 %reduce-scatter.5.cloned.1.call-start = ((), (), s32[]{:S(2)}) async-start(), calls=%async_computation.11 | async-start | bytes 11354112 | tf_op jit(solution)/shard_map/reduce_scatter | solution.py:257
  352.9 9.6 %copy-start.36 = (bf16[3,1024,64]{1,2,0:T(8,128)(2,1)S(1)}, bf16[3,1024,64]{1,2,0:T(8,128)(2,1)}, u32[]{:S(2)}) copy-start(bf16[3,1024,64]{1,2,0:T(8,128)(2,1)} %squeeze_reshape.14) | copy-start | bytes 1179652
  352.9 9.6 %copy-start.66 = (bf16[3,1024,64]{1,2,0:T(8,128)(2,1)S(1)}, bf16[3,1024,64]{1,2,0:T(8,128)(2,1)}, u32[]{:S(2)}) copy-start(bf16[3,1024,64]{1,2,0:T(8,128)(2,1)} %squeeze.172) | copy-start | bytes 1179652
  384.6 25.9 %copy-start.77 = (f32[768]{0:T(1024)S(1)}, f32[768]{0:T(1024)}, u32[]{:S(2)}) copy-start(f32[768]{0:T(1024)} %copy-done.76) | copy-start | bytes 9220
  384.6 25.9 %copy-start.83 = (f32[256]{0:T(256)S(1)}, f32[256]{0:T(256)}, u32[]{:S(2)}) copy-start(f32[256]{0:T(256)} %copy-done.82) | copy-start | bytes 3076
  384.6 25.9 %copy-start.87 = (f32[256]{0:T(256)S(1)}, f32[256]{0:T(256)}, u32[]{:S(2)}) copy-start(f32[256]{0:T(256)} %copy-done.86) | copy-start | bytes 3076
  384.6 24.3 %all-to-all-start.5 = ((bf16[4,3,256,192]{2,3,1,0:T(8,128)(2,1)}), bf16[4,3,256,192]{2,3,1,0:T(8,128)(2,1)}, u32[]{:S(2)}, u32[]{:S(2)}) async-start(bf16[4,3,256,192]{2,3,1,0:T(8,128)(2,1)} %bitcast.394), calls=%async_computation.5 | async-start | bytes 2359296 | tf_op jit(solution)/shard_map/all_to_all | solution.py:64
  424.5 17.9 %all-to-all-start.6 = ((bf16[4,1,256,192]{2,3,1,0:T(8,128)(2,1)}), bf16[4,1,256,192]{2,3,1,0:T(8,128)(2,1)}, u32[]{:S(2)}, u32[]{:S(2)}) async-start(bf16[4,1,256,192]{2,3,1,0:T(8,128)(2,1)} %bitcast.413), calls=%async_computation.6 | async-start | bytes 786432 | tf_op jit(solution)/shard_map/all_to_all | solution.py:53
  445.5 10.4 %copy-start.18 = (bf16[3,1024,64]{1,2,0:T(8,128)(2,1)S(1)}, bf16[3,1024,64]{1,2,0:T(8,128)(2,1)}, u32[]{:S(2)}) copy-start(bf16[3,1024,64]{1,2,0:T(8,128)(2,1)} %squeeze.153) | copy-start | bytes 1179652
  478.5 10.3 %copy-start.25 = (f32[256,768]{1,0:T(8,128)S(1)}, f32[256,768]{1,0:T(8,128)}, u32[]{:S(2)}) copy-start(f32[256,768]{1,0:T(8,128)} %copy-done.24) | copy-start | bytes 2359300
  478.5 20.3 %all-to-all-start.7 = ((bf16[4,3,256,192]{2,3,1,0:T(8,128)(2,1)}), bf16[4,3,256,192]{2,3,1,0:T(8,128)(2,1)}, u32[]{:S(2)}, u32[]{:S(2)}) async-start(bf16[4,3,256,192]{2,3,1,0:T(8,128)(2,1)} %bitcast.391), calls=%async_computation.7 | async-start | bytes 2359296 | tf_op jit(solution)/shard_map/all_to_all | solution.py:64
  482.9 225.9 %reduce-scatter.3.cloned.1.call-start = ((), (), s32[]{:S(2)}) async-start(), calls=%async_computation.10 | async-start | bytes 18653184 | tf_op jit(solution)/shard_map/reduce_scatter | solution.py:257
  (92 other events, 351.9 us)
Sparse Core Ops, SparseCore 0:
  17.3 109.2 all-gather.5
  130.1 108.8 all-gather.7
  347.3 149.2 reduce-scatter.4
  510.4 198.4 reduce-scatter.2
